TPU v7x, 128 devices: a whole 4x4x4 slice. The times are simulated.
128 devices in a mesh: gx: 16 (over z, x_lo, core), gy: 8 (over y, x_hi).
Axes of the slice: x: 4 (x_hi: 2, x_lo: 2; x = x_hi * 2 + x_lo), y: 4, z: 4, core: 2. Of those that a mesh axis runs over, the one named last changes fastest.
Arguments:
- adj_disp: float32 [3, 128, 128, 128], P(None, 'gx', 'gy'), may hold values from -6 to 6
- adj_veloc: float32 [3, 128, 128, 128], P(None, 'gx', 'gy'), may hold values from -6 to 6
- fwd_disp: float32 [3, 128, 128, 128], P(None, 'gx', 'gy'), may hold values from -6 to 6
- inv_mass: float32 [128, 128, 128], P('gx', 'gy'), may hold values from 0.5 to 2
- shear_mod: float32 [32, 32, 32], P('gx', 'gy'), may hold values from 0.5 to 2
- lame_mod: float32 [32, 32, 32], P('gx', 'gy'), may hold values from 0.5 to 2
- kernel_mu: float32 [125, 32768], P(None, ('gx', 'gy')), may hold values from -6 to 6
- kernel_kappa: float32 [125, 32768], P(None, ('gx', 'gy')), may hold values from -6 to 6
- chan_window: float32 [16, 1048576], P(None, ('gx', 'gy')), may hold values from -24 to 24
- chan_dir: float32 [3, 1048576], P(None, ('gx', 'gy')), may hold values from -6 to 6
- chan_local: float32 [3, 1048576], P(None, ('gx', 'gy')), may hold values from -1 to 1
- chan_part: int32 [1048576, 1], P(('gx', 'gy')), may hold values from 0 to 127; in each aligned block of 8192 rows (0 to 8191, 8192 to 16383, ...) at most 128 rows name the same one
- chan_elem: int32 [1048576], P(('gx', 'gy')), may hold values from 0 to 255
Outputs:
- adj_disp_new: float32 [3, 128, 128, 128], P(None, 'gx', 'gy')
- adj_veloc_new: float32 [3, 128, 128, 128], P(None, 'gx', 'gy')
- kernel_mu_new: float32 [125, 32768], P(None, ('gx', 'gy'))
- kernel_kappa_new: float32 [125, 32768], P(None, ('gx', 'gy'))
Inputs may be any that keep to these rules, and one draw needn't show every extreme that they name: `chan_part`: among the 8192 channels recorded by one partition, at most 128 lie in elements of any one owning partition, and in every draw some partition receives exactly 128 channels from some recording partition.
All inputs are finite; a program needn't handle non-finite values.
Results may differ from a plain program's by a relative error of at most 0.00005.
Values sent between devices are 32-bit elements; how exact they have to be, the bound alone decides.
No kernel may reach another device: no remote copies, remote signals or barrier semaphores. Data moves between devices by JAX's collectives and lax.ppermute only.
A program may use at most 128 MiB of HBM per device.

v0:
```python
import jax
import jax.numpy as jnp
import numpy as np
from jax import lax
from jax.sharding import PartitionSpec as P

NSAMP = 16


time_step = 0.05
highest = lax.Precision.HIGHEST


def shifted(x, axis, by):
    peers = lax.axis_size(axis)
    pairs = [(i, i + by) for i in range(peers) if 0 <= i + by < peers]
    return lax.ppermute(x, axis, pairs)


def gll_tables():
    gll_nodes = np.array([-1.0, -np.sqrt(3.0 / 7.0), 0.0, np.sqrt(3.0 / 7.0), 1.0])
    gll_weights = np.array([0.1, 49.0 / 90.0, 32.0 / 45.0, 49.0 / 90.0, 0.1])
    derivative = np.zeros((5, 5))
    for a in range(5):
        for p in range(5):
            summed = 0.0
            for m in range(5):
                if m != p:
                    factor = 1.0 / (gll_nodes[p] - gll_nodes[m])
                    for k in range(5):
                        if k != p and k != m:
                            factor = (
                                factor
                                * (gll_nodes[a] - gll_nodes[k])
                                / (gll_nodes[p] - gll_nodes[k])
                            )
                    summed = summed + factor
            derivative[a, p] = summed
    return (gll_nodes, gll_weights, derivative)


def time_filter():
    offsets = np.arange(NSAMP) - (NSAMP - 1) / 2.0
    cardinal = np.sin(np.pi * offsets) / (np.pi * offsets)
    values = cardinal * (0.5 + 0.5 * np.cos(np.pi * offsets / (NSAMP / 2.0)))
    return values / np.sum(values)


def lagrange_rows(points, gll_nodes):
    result_rows = []
    for p in range(5):
        value_row = jnp.ones_like(points)
        for m in range(5):
            if m != p:
                scale_term = float(1.0 / (gll_nodes[p] - gll_nodes[m]))
                value_row = value_row * ((points - float(gll_nodes[m])) * scale_term)
        result_rows.append(value_row)
    return jnp.stack(result_rows)


def open_axis(nodal_grid, axis_at, elem_count):
    turned = jnp.moveaxis(nodal_grid, axis_at, -1)
    leading = turned[..., : 4 * elem_count].reshape(turned.shape[:-1] + (elem_count, 4))
    trailing = turned[..., 4::4][..., None]
    joined = jnp.concatenate([leading, trailing], axis=-1)
    return jnp.moveaxis(joined, (-2, -1), (axis_at, axis_at + 1))


def fold_axis(pieces, axis_at, elem_count):
    turned = jnp.moveaxis(pieces, (axis_at, axis_at + 1), (-2, -1))
    widths = [(0, 0)] * (turned.ndim - 2)
    leading = jnp.pad(turned[..., :4], widths + [(0, 1), (0, 0)])
    trailing = jnp.pad(turned[..., 4], widths + [(1, 0)])
    leading = leading.at[..., 0].add(trailing)
    flat_view = leading.reshape(turned.shape[:-2] + (4 * (elem_count + 1),))[
        ..., : 4 * elem_count + 1
    ]
    return jnp.moveaxis(flat_view, -1, axis_at)


def to_elements(nodal_grid, ex_count, ey_count, ez_count):
    opened = open_axis(nodal_grid, 1, ex_count)
    opened = open_axis(opened, 3, ey_count)
    opened = open_axis(opened, 5, ez_count)
    opened = jnp.transpose(opened, (0, 2, 4, 6, 1, 3, 5))
    return opened.reshape(opened.shape[:4] + (ex_count * ey_count * ez_count,))


def from_elements(pieces, ex_count, ey_count, ez_count):
    shaped = pieces.reshape(pieces.shape[:4] + (ex_count, ey_count, ez_count))
    shaped = jnp.transpose(shaped, (0, 4, 1, 5, 2, 6, 3))
    shaped = fold_axis(shaped, 5, ez_count)
    shaped = fold_axis(shaped, 3, ey_count)
    return fold_axis(shaped, 1, ex_count)


def element_terms(adj_parts, fwd_parts, shear_vals, lame_vals, derivative, gll_weights):
    diff_matrix = jnp.asarray(derivative, jnp.float32)

    def gradient(pieces):
        along_x = jnp.einsum("ap,ipbce->iabce", diff_matrix, pieces, precision=highest)
        along_y = jnp.einsum("bp,iapce->iabce", diff_matrix, pieces, precision=highest)
        along_z = jnp.einsum("cp,iabpe->iabce", diff_matrix, pieces, precision=highest)
        return jnp.stack([along_x, along_y, along_z], axis=1)

    unit_tensor = jnp.eye(3, dtype=jnp.float32)[:, :, None, None, None, None]
    adj_grad = gradient(adj_parts)
    fwd_grad = gradient(fwd_parts)
    adj_strain = 0.5 * (adj_grad + jnp.swapaxes(adj_grad, 0, 1))
    fwd_strain = 0.5 * (fwd_grad + jnp.swapaxes(fwd_grad, 0, 1))
    adj_trace = adj_strain[0, 0] + adj_strain[1, 1] + adj_strain[2, 2]
    fwd_trace = fwd_strain[0, 0] + fwd_strain[1, 1] + fwd_strain[2, 2]
    stress = 2.0 * shear_vals * adj_strain + unit_tensor * (lame_vals * adj_trace)
    weight_vec = np.asarray(gll_weights)
    cubature = jnp.asarray(
        weight_vec[:, None, None] * weight_vec[None, :, None] * weight_vec[None, None, :],
        jnp.float32,
    )[..., None]
    weighted = stress * cubature
    divergence = jnp.einsum("pa,ipbce->iabce", diff_matrix, weighted[:, 0], precision=highest)
    divergence = divergence + jnp.einsum(
        "pb,iapce->iabce", diff_matrix, weighted[:, 1], precision=highest
    )
    divergence = divergence + jnp.einsum(
        "pc,iabpe->iabce", diff_matrix, weighted[:, 2], precision=highest
    )
    adj_dev = adj_strain - unit_tensor * (adj_trace / 3.0)
    fwd_dev = fwd_strain - unit_tensor * (fwd_trace / 3.0)
    shear_term = 2.0 * shear_vals * jnp.sum(adj_dev * fwd_dev, axis=(0, 1))
    bulk_term = (lame_vals + 2.0 / 3.0 * shear_vals) * adj_trace * fwd_trace
    return (divergence, shear_term, bulk_term)


def source_rows(records, element_ids, elem_total, gll_nodes):
    record_count = records.shape[1]
    block_rows = 4096

    def accumulate(running, turn_index):
        record_block = lax.dynamic_slice_in_dim(records, turn_index * block_rows, block_rows, 1)
        owners = lax.dynamic_slice_in_dim(element_ids, turn_index * block_rows, block_rows, 0)
        basis_x = lagrange_rows(record_block[3], gll_nodes)
        basis_y = lagrange_rows(record_block[4], gll_nodes)
        basis_z = lagrange_rows(record_block[5], gll_nodes)
        spread = (
            basis_x[:, None, None, :] * basis_y[None, :, None, :] * basis_z[None, None, :, :]
        ).reshape(125, block_rows)
        nodal_force = (record_block[0:3, None, :] * spread[None]).reshape(375, block_rows)
        return (running.at[owners].add(nodal_force.T), None)

    running, _ = lax.scan(
        accumulate,
        jnp.zeros((elem_total, 375), jnp.float32),
        jnp.arange(record_count // block_rows, dtype=jnp.int32),
    )
    return running


def local(
    adj_disp,
    adj_veloc,
    fwd_disp,
    inv_mass,
    shear_mod,
    lame_mod,
    kernel_mu,
    kernel_kappa,
    chan_window,
    chan_dir,
    chan_local,
    chan_part,
    chan_elem,
):
    ex_count, ey_count, ez_count = shear_mod.shape
    elem_count = ex_count * ey_count * ez_count
    depth_nodes = adj_disp.shape[3]
    size_strike = lax.axis_size("gx")
    size_dip = lax.axis_size("gy")
    devices = size_strike * size_dip
    gll_nodes, gll_weights, derivative = gll_tables()
    filter_row = jnp.asarray(time_filter(), jnp.float32)[None, :]
    strength = jnp.dot(
        filter_row, chan_window, precision=highest, preferred_element_type=jnp.float32
    )
    payload = jnp.concatenate([strength * chan_dir, chan_local], axis=0)
    target = chan_part[:, 0]
    channels = target.shape[0]
    capacity = 2 * channels // devices
    ranking = jnp.argsort(target, stable=True)
    sorted_target = target[ranking]
    counts = jnp.sum(
        (target[None, :] == jnp.arange(devices, dtype=jnp.int32)[:, None]).astype(jnp.int32), axis=1
    )
    starts = jnp.cumsum(counts) - counts
    slot_index = (
        sorted_target * capacity + jnp.arange(channels, dtype=jnp.int32) - starts[sorted_target]
    )
    outgoing = (
        jnp.zeros((6, devices * capacity), jnp.float32).at[:, slot_index].set(payload[:, ranking])
    )
    outgoing_ids = (
        jnp.zeros((1, devices * capacity), jnp.int32).at[0, slot_index].set(chan_elem[ranking])
    )
    incoming, incoming_ids = (
        lax.all_to_all(outgoing, ("gx", "gy"), split_axis=1, concat_axis=1, tiled=True),
        lax.all_to_all(outgoing_ids, ("gx", "gy"), split_axis=1, concat_axis=1, tiled=True),
    )
    source_all = source_rows(incoming, incoming_ids[0], elem_count, gll_nodes)
    source_parts = source_all.T.reshape(3, 5, 5, 5, elem_count)
    both_fields = jnp.concatenate([adj_disp, fwd_disp], axis=0)
    from_strike = shifted(both_fields[:, 0:1], "gx", -1)
    widened = jnp.concatenate([both_fields, from_strike], axis=1)
    from_dip = shifted(widened[:, :, 0:1], "gy", -1)
    extended = jnp.concatenate([widened, from_dip], axis=2)
    extended = jnp.pad(extended, ((0, 0), (0, 0), (0, 0), (0, 1)))
    element_parts = to_elements(extended, ex_count, ey_count, ez_count)
    divergence, shear_term, bulk_term = element_terms(
        element_parts[:3],
        element_parts[3:],
        shear_mod.reshape(-1),
        lame_mod.reshape(-1),
        derivative,
        gll_weights,
    )
    force_grid = from_elements(source_parts - divergence, ex_count, ey_count, ez_count)[
        ..., :depth_nodes
    ]
    back_dip = shifted(force_grid[:, :, -1:], "gy", 1)
    narrowed = force_grid[:, :, :-1].at[:, :, 0:1].add(back_dip)
    back_strike = shifted(narrowed[:, -1:], "gx", 1)
    assembled = narrowed[:, :-1].at[:, 0:1].add(back_strike)
    adj_veloc_new = adj_veloc + time_step * (inv_mass[None] * assembled)
    adj_disp_new = adj_disp + time_step * adj_veloc_new
    kernel_mu_new = kernel_mu + time_step * shear_term.reshape(125, elem_count)
    kernel_kappa_new = kernel_kappa + time_step * bulk_term.reshape(125, elem_count)
    return (adj_disp_new, adj_veloc_new, kernel_mu_new, kernel_kappa_new)


def solution(mesh):
    return jax.shard_map(
        local,
        mesh=mesh,
        in_specs=(
            P(None, "gx", "gy", None),
            P(None, "gx", "gy", None),
            P(None, "gx", "gy", None),
            P("gx", "gy", None),
            P("gx", "gy", None),
            P("gx", "gy", None),
            P(None, ("gx", "gy")),
            P(None, ("gx", "gy")),
            P(None, ("gx", "gy")),
            P(None, ("gx", "gy")),
            P(None, ("gx", "gy")),
            P(("gx", "gy"), None),
            P(("gx", "gy")),
        ),
        out_specs=(
            P(None, "gx", "gy", None),
            P(None, "gx", "gy", None),
            P(None, ("gx", "gy")),
            P(None, ("gx", "gy")),
        ),
        check_vma=False,
    )
```

profile of v0, /device:TPU:1, one launch (start us, length us, event | category | flops | bytes accessed | tf_op | source)
XLA Modules:
  0.0 624.9 jit_solution(9741986700197552234)
XLA Ops:
  7.6 7.5 %sort.17 = (s32[8192]{0:T(1024)}, s32[8192]{0:T(1024)S(1)}) sort(s32[8192]{0:T(1024)} %bitcast.166, s32[8192]{0:T(1024)S(1)} %iota.38), dimensions={0}, to_apply=%region_0.0 | sort | flops 106496 | bytes 131072 | tf_op jit(solution)/shard_map/jit(argsort)/sort | solution.py:188
  15.2 45.5 %gather_fusion = s32[8192]{0:T(1024)S(1)} fusion(s32[8192]{0:T(1024)S(1)} %bitcast.167, s32[8192]{0:T(1024)S(1)} %fusion.27), kind=kCustom, calls=%fused_computation | custom fusion | bytes 98304 | tf_op jit(solution)/shard_map/gather | solution.py:189
  60.8 48.9 %gather_fusion.1 = s32[8192]{0:T(1024)S(1)} fusion(s32[128]{0:T(128)S(1)} %sub.41, s32[8192]{0:T(1024)S(1)} %broadcast_clamp_fusion), kind=kCustom, calls=%fused_computation.1 | custom fusion | bytes 98304 | tf_op jit(solution)/shard_map/gather | solution.py:195
  110.5 45.5 %gather_fusion.2 = s32[8192]{0:T(1024)S(1)} fusion(s32[8192]{0:T(1024)S(1)} %copy-done.3, s32[8192]{0:T(1024)S(1)} %fusion.27), kind=kCustom, calls=%fused_computation.2 | custom fusion | bytes 98304 | tf_op jit(solution)/shard_map/gather | solution.py:201
  156.0 31.0 %scatter_custom_fusion.2 = s32[16384]{0:T(1024)} fusion(s32[8192]{0:T(1024)S(1)} %broadcast_select_fusion, s32[8192]{0:T(1024)S(1)} %gather_fusion.2, s32[]{:T(128)} %constant.284.clone.1), kind=kCustom, calls=%fused_computation.119 | custom fusion | bytes 65540
  187.1 10.6 %all-to-all-start = ((s32[1,128,128]{2,0,1:T(1,128)}), s32[1,128,128]{2,0,1:T(1,128)S(1)}, u32[]{:S(2)}, u32[]{:S(2)}) async-start(s32[1,128,128]{2,0,1:T(1,128)} %bitcast.7), calls=%async_computation | async-start | bytes 131072 | tf_op jit(solution)/shard_map/all_to_all | solution.py:205
  202.9 70.4 %scatter_custom_fusion.1 = f32[6,16384]{0,1:T(8,128)} fusion(s32[8192]{0:T(1024)S(1)} %bitcast.182, f32[6,8192]{0,1:T(8,128)} %copy.232, s32[8192]{0:T(1024)S(1)} %fusion.27, f32[]{:T(128)} %constant.285.clone.1), kind=kCustom, calls=%fused_computation.39 | custom fusion | bytes 393728 | tf_op jit(solution)/shard_map/scatter | solution.py:198
  273.3 6.1 copy.233
  282.1 23.6 %slice.311 = f32[6,2,5,4,5,32]{5,3,4,2,1,0:T(4,128)} slice(f32[6,2,5,4,5,129]{5,3,4,2,1,0:T(4,128)S(1)} %maximum_bitcast_fusion.2), slice={[0:6:1], [0:2:1], [0:5:1], [0:4:1], [0:5:1], [4:129:4]} | slice | bytes 307200 | tf_op jit(solution)/shard_map/slice | solution.py:64
  305.8 22.3 %reshape.422 = f32[6,2,5,4,5,32,4]{6,5,3,4,2,1,0:T(8,128)} reshape(f32[6,2,5,4,5,128]{5,3,4,2,1,0:T(4,128)S(1)} %slice.354) | data formatting | bytes 1228800 | tf_op jit(solution)/shard_map/reshape | solution.py:63
  328.1 13.1 %copy.237 = f32[6,2,5,4,5,32,4]{5,3,6,4,2,1,0:T(4,128)S(1)} copy(f32[6,2,5,4,5,32,4]{6,5,3,4,2,1,0:T(8,128)} %reshape.422) | data formatting | bytes 1228800 | tf_op jit(solution)/shard_map/reshape | solution.py:63
  363.1 11.6 %all-to-all-start.1 = ((f32[6,128,128]{2,0,1:T(8,128)}), f32[6,128,128]{2,0,1:T(8,128)S(1)}, u32[]{:S(2)}, u32[]{:S(2)}) async-start(f32[6,128,128]{2,0,1:T(8,128)} %copy.233), calls=%async_computation.1 | async-start | bytes 1048576 | tf_op jit(solution)/shard_map/all_to_all | solution.py:204
  377.9 10.8 %all-to-all-done.1 = f32[6,128,128]{2,0,1:T(8,128)S(1)} async-done(((f32[6,128,128]{2,0,1:T(8,128)}), f32[6,128,128]{2,0,1:T(8,128)S(1)}, u32[]{:S(2)}, u32[]{:S(2)}) %all-to-all-start.1) | async-done | bytes 393248 | tf_op jit(solution)/shard_map/all_to_all | solution.py:204
  388.8 201.8 %while.18 = (s32[]{:T(128)}, f32[256,375]{1,0:T(8,128)S(1)}, s32[4]{0:T(128)S(1)}, s32[16384]{0:T(1024)S(1)}, f32[6,16384]{1,0:T(8,128)S(1)}, /*index=5*/s32[]{:...) while((s32[]{:T(128)}, f32[256,375]{1,0:T(8,128)S(1)}, s32[4]{0:T(128)S(1)}, ...), condition=%wide.region_7.8_spmd, body=%wide.region_5.7_spmd.sunk | while | flops 4153353 | bytes 59392240 | solution.py:150
  395.3 3.4 broadcast_multiply_fusion.10
  398.7 6.1 mul.1256
  404.7 6.5 %copy.328 = f32[4096,375]{1,0:T(8,128)} copy(f32[4096,375]{0,1:T(8,128)} %bitcast.168) | data formatting | bytes 12288000 | tf_op jit(solution)/shard_map/while/body/eval_jaxpr/transpose | solution.py:148
  411.3 27.8 %scatter_fusion = f32[256,375]{1,0:T(8,128)S(1)} fusion(f32[256,375]{1,0:T(8,128)S(1)} %get-tuple-element.301, s32[4096]{0:T(1024)S(1)} %compare_select_fusion.5, f32[4096,375]{1,0:T(8,128)} %copy.328), kind=kCustom, calls=%fused_computation.4.clone.1 | custom fusion | flops 1536000 | bytes 18448384 | tf_op jit(solution)/shard_map/while/body/eval_jaxpr/scatter-add | solution.py:148
  445.5 3.4 broadcast_multiply_fusion.10
  448.9 6.1 mul.1256
  455.0 6.5 %copy.328 = f32[4096,375]{1,0:T(8,128)} copy(f32[4096,375]{0,1:T(8,128)} %bitcast.168) | data formatting | bytes 12288000 | tf_op jit(solution)/shard_map/while/body/eval_jaxpr/transpose | solution.py:148
  461.5 28.0 %scatter_fusion = f32[256,375]{1,0:T(8,128)S(1)} fusion(f32[256,375]{1,0:T(8,128)S(1)} %get-tuple-element.301, s32[4096]{0:T(1024)S(1)} %compare_select_fusion.5, f32[4096,375]{1,0:T(8,128)} %copy.328), kind=kCustom, calls=%fused_computation.4.clone.1 | custom fusion | flops 1536000 | bytes 18448384 | tf_op jit(solution)/shard_map/while/body/eval_jaxpr/scatter-add | solution.py:148
  499.4 6.1 mul.1256
  505.5 6.5 %copy.328 = f32[4096,375]{1,0:T(8,128)} copy(f32[4096,375]{0,1:T(8,128)} %bitcast.168) | data formatting | bytes 12288000 | tf_op jit(solution)/shard_map/while/body/eval_jaxpr/transpose | solution.py:148
  512.0 28.0 %scatter_fusion = f32[256,375]{1,0:T(8,128)S(1)} fusion(f32[256,375]{1,0:T(8,128)S(1)} %get-tuple-element.301, s32[4096]{0:T(1024)S(1)} %compare_select_fusion.5, f32[4096,375]{1,0:T(8,128)} %copy.328), kind=kCustom, calls=%fused_computation.4.clone.1 | custom fusion | flops 1536000 | bytes 18448384 | tf_op jit(solution)/shard_map/while/body/eval_jaxpr/scatter-add | solution.py:148
  546.6 3.4 broadcast_multiply_fusion.10
  550.0 6.1 mul.1256
  556.0 6.5 %copy.328 = f32[4096,375]{1,0:T(8,128)} copy(f32[4096,375]{0,1:T(8,128)} %bitcast.168) | data formatting | bytes 12288000 | tf_op jit(solution)/shard_map/while/body/eval_jaxpr/transpose | solution.py:148
  562.6 28.0 %scatter_fusion = f32[256,375]{1,0:T(8,128)S(1)} fusion(f32[256,375]{1,0:T(8,128)S(1)} %get-tuple-element.301, s32[4096]{0:T(1024)S(1)} %compare_select_fusion.5, f32[4096,375]{1,0:T(8,128)} %copy.328), kind=kCustom, calls=%fused_computation.4.clone.1 | custom fusion | flops 1536000 | bytes 18448384 | tf_op jit(solution)/shard_map/while/body/eval_jaxpr/scatter-add | solution.py:148
  596.3 7.4 %copy.256 = f32[3,2,5,4,5,33,4]{6,5,3,4,2,1,0:T(8,128)} copy(f32[3,2,5,4,5,33,4]{5,3,1,0,4,2,6:T(4,128)S(1)} %fusion.23) | data formatting | bytes 633600 | tf_op jit(solution)/shard_map/scatter-add | solution.py:74
  603.8 7.5 %reshape.426 = f32[3,2,5,4,5,132]{5,3,4,2,1,0:T(4,128)S(1)} reshape(f32[3,2,5,4,5,33,4]{6,5,3,4,2,1,0:T(8,128)} %copy.256) | data formatting | bytes 633600 | tf_op jit(solution)/shard_map/reshape | solution.py:75
  616.7 5.1 collective-permute-start.3
  (214 shorter events, 80.7 us)
Async XLA Ops:
  0.6 197.2 %copy-start = (f32[16,8192]{1,0:T(8,128)S(1)}, f32[16,8192]{1,0:T(8,128)}, u32[]{:S(2)}) copy-start(f32[16,8192]{1,0:T(8,128)} %param.36) | copy-start | bytes 1572868
  0.6 14.5 %copy-start.2 = (s32[8192,1]{0,1:T(1,128)S(1)}, s32[8192,1]{0,1:T(1,128)}, u32[]{:S(2)}) copy-start(s32[8192,1]{0,1:T(1,128)} %param.39) | copy-start | bytes 98308
  2.6 196.3 %collective-permute-start = (f32[6,1,16,128]{3,2,1,0:T(8,128)S(1)}, f32[6,1,16,128]{3,2,1,0:T(8,128)S(1)}, u32[]{:S(2)}, u32[]{:S(2)}) collective-permute-start(f32[6,1,16,128]{3,2,1,0:T(8,128)S(1)} %slice.351), channel_id=1, source_target_pairs={{8,0},{16,8},{24,16},{32,24},{40,32},{48,40},{56,48},{64,56},{72,6... | collective-permute-start | bytes 147464 | tf_op jit(solution)/shard_map/ppermute | solution.py:17
  60.8 49.0 %copy-start.28 = (s32[2]{0:T(128)S(1)}, s32[2]{0:T(128)}, u32[]{:S(2)}) copy-start(s32[2]{0:T(128)} %constant.322) | copy-start | bytes 28
  60.8 49.2 %copy-start.27 = (s32[2]{0:T(128)S(1)}, s32[2]{0:T(128)}, u32[]{:S(2)}) copy-start(s32[2]{0:T(128)} %constant.319) | copy-start | bytes 28
  110.5 87.2 %copy-start.24 = (f32[2,4,32]{2,1,0:T(4,128)S(1)}, f32[2,4,32]{2,1,0:T(4,128)}, u32[]{:S(2)}) copy-start(f32[2,4,32]{2,1,0:T(4,128)} %param.33) | copy-start | bytes 3076
  110.5 87.3 %copy-start.25 = (f32[2,4,32]{2,1,0:T(4,128)S(1)}, f32[2,4,32]{2,1,0:T(4,128)}, u32[]{:S(2)}) copy-start(f32[2,4,32]{2,1,0:T(4,128)} %param.32) | copy-start | bytes 3076
  110.5 87.4 %copy-start.26 = (f32[16,1]{0,1:T(1,128)S(1)}, f32[16,1]{0,1:T(1,128)}, u32[]{:S(2)}) copy-start(f32[16,1]{0,1:T(1,128)} %constant.327) | copy-start | bytes 196
  110.5 87.8 %copy-start.17 = (f32[3,8192]{1,0:T(4,128)S(1)}, f32[3,8192]{1,0:T(4,128)}, u32[]{:S(2)}) copy-start(f32[3,8192]{1,0:T(4,128)} %param.37) | copy-start | bytes 294916
  110.5 87.8 %copy-start.18 = (f32[3,8192]{1,0:T(4,128)S(1)}, f32[3,8192]{1,0:T(4,128)}, u32[]{:S(2)}) copy-start(f32[3,8192]{1,0:T(4,128)} %param.38) | copy-start | bytes 294916
  187.1 176.1 %all-to-all-start = ((s32[1,128,128]{2,0,1:T(1,128)}), s32[1,128,128]{2,0,1:T(1,128)S(1)}, u32[]{:S(2)}, u32[]{:S(2)}) async-start(s32[1,128,128]{2,0,1:T(1,128)} %bitcast.7), calls=%async_computation | async-start | bytes 131072 | tf_op jit(solution)/shard_map/all_to_all | solution.py:205
  198.9 81.1 %collective-permute-start.1 = (f32[6,9,1,128]{3,2,1,0:T(1,128)S(1)}, f32[6,9,1,128]{3,2,1,0:T(1,128)S(1)}, u32[]{:S(2)}, u32[]{:S(2)}) collective-permute-start(f32[6,9,1,128]{3,2,1,0:T(1,128)S(1)} %pad_maximum_fusion.3), channel_id=1, source_target_pairs={{1,0},{2,1},{3,2},{4,3},{5,4},{6,5},{7,6},{9,8},{10,9},{11,10},{12... | collective-permute-start | bytes 82952 | tf_op jit(solution)/shard_map/ppermute | solution.py:17
  273.3 6.1 copy-start.20
  343.6 3.9 copy-start.12
  354.5 2.1 copy-start.7
  360.3 1.3 copy-start.4
  363.1 25.6 %all-to-all-start.1 = ((f32[6,128,128]{2,0,1:T(8,128)}), f32[6,128,128]{2,0,1:T(8,128)S(1)}, u32[]{:S(2)}, u32[]{:S(2)}) async-start(f32[6,128,128]{2,0,1:T(8,128)} %copy.233), calls=%async_computation.1 | async-start | bytes 1048576 | tf_op jit(solution)/shard_map/all_to_all | solution.py:204
  388.8 202.1 %copy-start.13 = (f32[5,5,1,1,1]{1,0,4,3,2:T(8,128)S(1)}, f32[5,5,1,1,1]{1,0,4,3,2:T(8,128)}, u32[]{:S(2)}) copy-start(f32[5,5,1,1,1]{1,0,4,3,2:T(8,128)} %constant.328) | copy-start | bytes 304
  590.6 1.3 copy-start.6
  613.2 2.6 copy-start.10
  613.2 2.6 copy-start.11
  613.2 2.6 copy-start.19
  613.2 2.6 copy-start.23
  613.3 3.3 copy-start.8
  613.5 8.3 %copy-start.16 = (f32[125,256]{1,0:T(8,128)S(1)}, f32[125,256]{1,0:T(8,128)}, u32[]{:S(2)}) copy-start(f32[125,256]{1,0:T(8,128)} %param.34) | copy-start | bytes 384004
  613.5 8.3 %copy-start.22 = (f32[256]{0:T(256)S(1)}, f32[256]{0:T(256)}, u32[]{:S(2)}) copy-start(f32[256]{0:T(256)} %get-tuple-element.224) | copy-start | bytes 3076
  613.6 9.3 %copy-start.9 = (f32[3,8,16,128]{3,2,1,0:T(8,128)S(1)}, f32[3,8,16,128]{3,2,1,0:T(8,128)}, u32[]{:S(2)}) copy-start(f32[3,8,16,128]{3,2,1,0:T(8,128)} %param.28) | copy-start | bytes 589828
  613.6 9.3 %copy-start.14 = (f32[8,16,128]{2,0,1:T(8,128)S(1)}, f32[8,16,128]{2,0,1:T(8,128)}, u32[]{:S(2)}) copy-start(f32[8,16,128]{2,0,1:T(8,128)} %copy.230) | copy-start | bytes 196612
  613.6 9.3 %copy-start.15 = (f32[3,8,16,128]{3,2,1,0:T(8,128)S(1)}, f32[3,8,16,128]{3,2,1,0:T(8,128)}, u32[]{:S(2)}) copy-start(f32[3,8,16,128]{3,2,1,0:T(8,128)} %param.29) | copy-start | bytes 589828
  613.6 3.1 collective-permute-start.2
  616.6 7.9 %copy-start.1 = (f32[16,8192]{1,0:T(8,128)S(1)}, f32[16,8192]{1,0:T(8,128)}, u32[]{:S(2)}) copy-start(f32[16,8192]{1,0:T(8,128)} %param.36) | copy-start | bytes 1572868
  616.7 6.0 collective-permute-start.3
  (3 other events, 2.6 us)
where the time goes:
time: 637 us; the launch traced here: 625 us
  local copies, waits for them, and re-layouts  410 us (64%)
  other arithmetic  154 us (24%)
  starting transfers between devices  33.9 us (5%)
  waiting for transfers between devices  11.1 us (2%)
  matrix products  10.7 us (2%)
    scatter-add x4, other arithmetic, accumulate(): return (running.at[owners].add(nodal_force.T), None)  112 us
    scatter x1, local copies, waits for them, and re-layouts, local(): jnp.zeros((6, devices * capacity), jnp.float32).at[:, slot_index]  70.4 us
    gather x1, local copies, waits for them, and re-layouts, local(): starts[sorted_target]  48.9 us
    gather x1, local copies, waits for them, and re-layouts, local(): sorted_target = target[ranking]  45.5 us
    gather x1, local copies, waits for them, and re-layouts, local(): chan_elem[ranking]  45.5 us
    unnamed x65, local copies, waits for them, and re-layouts  37.7 us
    reshape x4, local copies, waits for them, and re-layouts, open_axis(): turned[..., :4 * elem_count].reshape(turned.shape[:-1] + (elem_count, 4))  36.1 us
    transpose x4, local copies, waits for them, and re-layouts, accumulate(): return (running.at[owners].add(nodal_force.T), None)  26.2 us
  transfers between devices with their start and end apart: 6, of which 3 were waited for; matrix products, arithmetic and copies ran while one was open for 56% of the time, Pallas kernels for 0%

commit v1 on v0

v1 whole, which is shorter than its diff:
```python
import jax
import jax.numpy as jnp
import numpy as np
from jax import lax
from jax.experimental import pallas as pl
from jax.experimental.pallas import tpu as pltpu
from jax.sharding import PartitionSpec as P

NSAMP = 16
time_step = 0.05
f32, bf16, i32 = jnp.float32, jnp.bfloat16, jnp.int32

EX, EY, EZ = 2, 4, 32
NCH = 8192
NDEV = 128
CAP = 128
ELEMS = EX * EY * EZ
LIMIT = 56 * 1024 * 1024


def gll_tables():
    gll_nodes = np.array([-1.0, -np.sqrt(3.0 / 7.0), 0.0, np.sqrt(3.0 / 7.0), 1.0])
    gll_weights = np.array([0.1, 49.0 / 90.0, 32.0 / 45.0, 49.0 / 90.0, 0.1])
    derivative = np.zeros((5, 5))
    for a in range(5):
        for p in range(5):
            summed = 0.0
            for m in range(5):
                if m != p:
                    factor = 1.0 / (gll_nodes[p] - gll_nodes[m])
                    for k in range(5):
                        if k != p and k != m:
                            factor = (
                                factor
                                * (gll_nodes[a] - gll_nodes[k])
                                / (gll_nodes[p] - gll_nodes[k])
                            )
                    summed = summed + factor
            derivative[a, p] = summed
    return (gll_nodes, gll_weights, derivative)


def time_filter():
    offsets = np.arange(NSAMP) - (NSAMP - 1) / 2.0
    cardinal = np.sin(np.pi * offsets) / (np.pi * offsets)
    values = cardinal * (0.5 + 0.5 * np.cos(np.pi * offsets / (NSAMP / 2.0)))
    return values / np.sum(values)


nodes, weights, deriv = gll_tables()


def halves(matrix):
    matrix = np.asarray(matrix, np.float32)
    top = matrix.astype(jnp.bfloat16)
    low = (matrix - top.astype(np.float32)).astype(jnp.bfloat16)
    return top, low


def padded_row(c, a, b):
    return c * 40 + a * 8 + b


def build_tables():
    select = np.zeros((EY * 128, 5 * 128), np.float32)
    for ey in range(EY):
        for c in range(5):
            for ez in range(EZ):
                if 4 * ez + c < 128:
                    select[ey * 128 + 4 * ez + c, c * 128 + ey * 32 + ez] = 1.0
    grad = np.zeros((384, 208))
    div = np.zeros((208, 384))
    for a in range(5):
        for b in range(5):
            for c in range(5):
                row = 25 * a + 5 * b + c
                for p in range(5):
                    grad[row, padded_row(c, p, b)] += deriv[a, p]
                    grad[128 + row, padded_row(c, a, p)] += deriv[b, p]
                    grad[256 + row, padded_row(p, a, b)] += deriv[c, p]
                    out = padded_row(c, a, b)
                    div[out, 25 * p + 5 * b + c] += (
                        deriv[p, a] * weights[p] * weights[b] * weights[c]
                    )
                    div[out, 128 + 25 * a + 5 * p + c] += (
                        deriv[p, b] * weights[a] * weights[p] * weights[c]
                    )
                    div[out, 256 + 25 * a + 5 * b + p] += (
                        deriv[p, c] * weights[a] * weights[b] * weights[p]
                    )
    place = np.zeros((608, 384), np.float32)
    for i in range(3):
        for a in range(5):
            for b in range(5):
                for c in range(5):
                    bc = 5 * b + c
                    at = (i * 5 + a) * 24 + bc if bc < 24 else 360 + i * 5 + a
                    place[i * 200 + padded_row(c, a, b), at] = 1.0
    upper = np.zeros((256, 384), np.float32)
    upper[:, :256] = np.arange(256)[:, None] < np.arange(256)[None, :]
    upper[:, 256:] = 1.0
    return select, grad, div, place, upper


SELECT, GRAD, DIV, PLACE, UPPER = build_tables()


def shifted(x, axis, by):
    peers = lax.axis_size(axis)
    pairs = [(i, i + by) for i in range(peers) if 0 <= i + by < peers]
    return lax.ppermute(x, axis, pairs)


def dot(x, y):
    return jnp.dot(x, y, preferred_element_type=f32)


def dot_nt(x, y):
    return lax.dot_general(x, y, (((1,), (1,)), ((), ())), preferred_element_type=f32)


def split2(x):
    top = x.astype(bf16)
    return top, (x - top.astype(f32)).astype(bf16)


PACK_CHUNK = 512


def pack_kernel(
    win_ref, dir_ref, loc_ref, part_ref, elem_ref, coef_ref, upper_ref, out_ref, key_ref, a_ref, acc_ref
):
    upper = upper_ref[...]

    def rank_step(at, base):
        span = pl.ds(pl.multiple_of(at * 256, 256), 256)
        target = part_ref[:, span]
        same = lax.broadcasted_iota(i32, (NDEV, 256), 0) == target
        running = dot(jnp.where(same, 1.0, 0.0).astype(bf16), upper)
        before = running[:, :256] + jnp.concatenate([base, base], axis=1)
        rank = jnp.sum(jnp.where(same, before, 0.0), axis=0, keepdims=True)
        key_ref[:, span] = rank.astype(i32) + (target >> 6) * CAP
        return base + running[:, 256:]

    lax.fori_loop(0, NCH // 256, rank_step, jnp.zeros((NDEV, 128), f32), unroll=4)
    acc_ref[...] = jnp.zeros_like(acc_ref)
    coef = coef_ref[:, 0:1]

    def fill_step(at, carry):
        span = pl.ds(pl.multiple_of(at * PACK_CHUNK, PACK_CHUNK), PACK_CHUNK)
        strength = jnp.sum(win_ref[:, span] * coef, axis=0, keepdims=True)
        force = strength * dir_ref[:, span]
        where_at = loc_ref[:, span]
        force_low = force - force.astype(bf16).astype(f32)
        where_low = where_at - where_at.astype(bf16).astype(f32)
        elem = elem_ref[:, span].astype(f32)
        rows = [force[k : k + 1] for k in range(3)] + [where_at[k : k + 1] for k in range(3)]
        rows += [force_low[k : k + 1] for k in range(3)] + [where_low[k : k + 1] for k in range(3)]
        rows += [elem]
        mask = lax.broadcasted_iota(i32, (64, PACK_CHUNK), 0) == (part_ref[:, span] & 63)
        for k, row in enumerate(rows):
            a_ref[k * 64 : (k + 1) * 64, :] = jnp.where(mask, row, 0.0).astype(bf16)
        slot = lax.broadcasted_iota(i32, (256, PACK_CHUNK), 0) == key_ref[:, span]
        acc_ref[...] += dot_nt(a_ref[...], jnp.where(slot, 1.0, 0.0).astype(bf16))
        return carry

    lax.fori_loop(0, NCH // PACK_CHUNK, fill_step, 0)
    for half in range(2):
        lanes = slice(half * 128, (half + 1) * 128)
        for v in range(6):
            out_ref[pl.ds(half * 512 + v, 64, stride=8), :] = (
                acc_ref[v * 64 : (v + 1) * 64, lanes] + acc_ref[(6 + v) * 64 : (7 + v) * 64, lanes]
            )
        out_ref[pl.ds(half * 512 + 6, 64, stride=8), :] = acc_ref[12 * 64 : 13 * 64, lanes]
        out_ref[pl.ds(half * 512 + 7, 64, stride=8), :] = jnp.zeros((64, 128), f32)


def pack(chan_window, chan_dir, chan_local, part_row, elem_row):
    coef = np.tile(time_filter().astype(np.float32)[:, None], (1, 128))
    return pl.pallas_call(
        pack_kernel,
        out_shape=jax.ShapeDtypeStruct((NDEV * 8, 128), f32),
        scratch_shapes=[
            pltpu.VMEM((1, NCH), i32),
            pltpu.VMEM((13 * 64, PACK_CHUNK), bf16),
            pltpu.VMEM((13 * 64, 256), f32),
        ],
        compiler_params=pltpu.CompilerParams(vmem_limit_bytes=LIMIT),
        cost_estimate=pl.CostEstimate(
            flops=5 * 10**9, bytes_accessed=1500000, transcendentals=0
        ),
        name="pack",
    )(chan_window, chan_dir, chan_local, part_row, elem_row, jnp.asarray(coef), jnp.asarray(UPPER, bf16))


def element_kernel(
    adj_ref,
    fwd_ref,
    strike_ref,
    dip_ref,
    shear_ref,
    lame_ref,
    mu_ref,
    kappa_ref,
    select_ref,
    grad_ref,
    div_ref,
    mu_out,
    kappa_out,
    force_out,
    n_ref,
    x_ref,
    u_ref,
    g_ref,
    t_ref,
):
    for f in range(6):
        source = adj_ref if f < 3 else fwd_ref
        for x in range(9):
            base = (f * 9 + x) * 24
            if x < 8:
                n_ref[base : base + 16, :] = source[f % 3, x]
            else:
                n_ref[base : base + 16, :] = strike_ref[f]
            n_ref[base + 16 : base + 24, :] = jnp.zeros((8, 128), f32)
            n_ref[base + 16 : base + 17, :] = dip_ref[f, x : x + 1, :]
    for f in range(6):
        for ex in range(EX):
            for a in range(5):
                for ey in range(EY):
                    base = (f * 9 + 4 * ex + a) * 24 + 4 * ey
                    at = (f * 2 + ex) * 40 + a * 8
                    x_ref[at : at + 8, ey * 128 : (ey + 1) * 128] = n_ref[base : base + 8, :]
    whole = x_ref[...]
    top, rest = whole.astype(bf16), None
    rest = whole - top.astype(f32)
    mid = rest.astype(bf16)
    low = (rest - mid.astype(f32)).astype(bf16)
    select = select_ref[...]
    opened = (dot(low, select) + dot(mid, select)) + dot(top, select)
    for block in range(12):
        for c in range(5):
            u_ref[c * 40 : (c + 1) * 40, block * 128 : (block + 1) * 128] = opened[
                block * 40 : (block + 1) * 40, c * 128 : (c + 1) * 128
            ]
    u_ref[200:208, :] = jnp.zeros((8, 1536), f32)
    top, low = split2(u_ref[...])
    both = dot(grad_ref[...], top)
    g_ref[...] = both[:384] + (both[384:] + dot(grad_ref[:384, :], low))
    for ex in range(EX):
        lanes = slice(ex * 128, (ex + 1) * 128)
        shear = shear_ref[:, lanes]
        lame = lame_ref[:, lanes]
        bulk = lame + 2.0 / 3.0 * shear
        for tile in range(16):
            rows = slice(tile * 8, tile * 8 + 8)

            def grad(f, i, j):
                block = (f * 3 + i) * 2 + ex
                return g_ref[j * 128 + tile * 8 : j * 128 + tile * 8 + 8, block * 128 : (block + 1) * 128]

            strains = []
            for f in range(2):
                strain = {}
                for i in range(3):
                    strain[i, i] = grad(f, i, i)
                    for j in range(i):
                        strain[i, j] = 0.5 * (grad(f, i, j) + grad(f, j, i))
                        strain[j, i] = strain[i, j]
                strains.append(strain)
            adj, fwd = strains
            adj_trace = adj[0, 0] + adj[1, 1] + adj[2, 2]
            fwd_trace = fwd[0, 0] + fwd[1, 1] + fwd[2, 2]
            twice = 2.0 * shear
            pressure = lame * adj_trace
            for i in range(3):
                for j in range(3):
                    value = twice * adj[i, j]
                    if i == j:
                        value = value + pressure
                    block = i * 2 + ex
                    t_ref[j * 128 + tile * 8 : j * 128 + tile * 8 + 8, block * 128 : (block + 1) * 128] = value
            traces = adj_trace * fwd_trace
            product = (
                adj[0, 0] * fwd[0, 0] + adj[1, 1] * fwd[1, 1] + adj[2, 2] * fwd[2, 2]
            ) - traces * (1.0 / 3.0)
            product = product + 2.0 * (
                adj[1, 0] * fwd[1, 0] + adj[2, 0] * fwd[2, 0] + adj[2, 1] * fwd[2, 1]
            )
            count = 8 if tile < 15 else 5
            rows = slice(tile * 8, tile * 8 + count)
            mu_out[rows, lanes] = mu_ref[rows, lanes] + (time_step * twice * product)[:count]
            kappa_out[rows, lanes] = kappa_ref[rows, lanes] + (time_step * bulk * traces)[:count]
    top, low = split2(t_ref[...])
    both = dot(div_ref[...], top)
    result = both[:208] + (both[208:] + dot(div_ref[:208, :], low))
    for i in range(3):
        force_out[i * 200 : (i + 1) * 200, :] = result[:200, i * 256 : (i + 1) * 256]


def element_terms(adj, fwd, strike, dip, shear, lame, mu, kappa):
    grad = np.concatenate(halves(GRAD), axis=0)
    div = np.concatenate(halves(DIV), axis=0)
    return pl.pallas_call(
        element_kernel,
        out_shape=[
            jax.ShapeDtypeStruct((125, ELEMS), f32),
            jax.ShapeDtypeStruct((125, ELEMS), f32),
            jax.ShapeDtypeStruct((600, ELEMS), f32),
        ],
        scratch_shapes=[
            pltpu.VMEM((6 * 9 * 24, 128), f32),
            pltpu.VMEM((480, 512), f32),
            pltpu.VMEM((208, 1536), f32),
            pltpu.VMEM((384, 1536), f32),
            pltpu.VMEM((384, 768), f32),
        ],
        compiler_params=pltpu.CompilerParams(vmem_limit_bytes=LIMIT),
        cost_estimate=pl.CostEstimate(
            flops=5 * 10**9, bytes_accessed=5000000, transcendentals=0
        ),
        name="element_terms",
    )(adj, fwd, strike, dip, shear, lame, mu, kappa, jnp.asarray(SELECT, bf16), jnp.asarray(grad), jnp.asarray(div))


def source_kernel(
    inc_ref,
    div_ref,
    place_ref,
    back_ref,
    main_out,
    dip_out,
    strike_out,
    gx_ref,
    yz_ref,
    a_ref,
    b_ref,
    acc_ref,
    z_ref,
    f_ref,
):
    acc_ref[...] = jnp.zeros_like(acc_ref)

    def basis(points):
        gaps = [points - float(np.float32(nodes[m])) for m in range(5)]
        result = []
        for p in range(5):
            scale = 1.0
            value = None
            for m in range(5):
                if m != p:
                    scale = scale / (nodes[p] - nodes[m])
                    value = gaps[m] if value is None else value * gaps[m]
            result.append(value * float(scale))
        return result

    def step(at, carry):
        base = pl.multiple_of(at * 64, 64)
        values = [inc_ref[pl.ds(base + v, 8, stride=8), :] for v in range(7)]
        lx, ly, lz = basis(values[3]), basis(values[4]), basis(values[5])
        for i in range(3):
            for a in range(5):
                gx_ref[pl.ds(i * 5 + a, 8, stride=16), :] = values[i] * lx[a]
        gx_ref[pl.ds(15, 8, stride=16), :] = jnp.zeros((8, 128), f32)
        for b in range(5):
            for c in range(5):
                yz_ref[pl.ds(b * 5 + c, 8, stride=32), :] = ly[b] * lz[c]
        index = values[6].astype(i32)
        for s in range(8):
            yz = yz_ref[s * 32 : s * 32 + 24, :]
            parts = [gx_ref[s * 16 + k : s * 16 + k + 1, :] * yz for k in range(15)]
            parts.append(gx_ref[s * 16 : s * 16 + 16, :] * yz_ref[s * 32 + 24 : s * 32 + 25, :])
            parts.append(jnp.zeros((8, 128), f32))
            whole = jnp.concatenate(parts, axis=0)
            top, low = split2(whole)
            lanes = slice(s * 128, (s + 1) * 128)
            a_ref[0:384, lanes] = top
            a_ref[384:768, lanes] = low
            here = lax.broadcasted_iota(i32, (ELEMS, 128), 0) == index[s : s + 1, :]
            b_ref[:, lanes] = jnp.where(here, 1.0, 0.0).astype(bf16)
        acc_ref[...] += dot_nt(a_ref[...], b_ref[...])
        return carry

    lax.fori_loop(0, 16, step, 0)
    source = acc_ref[0:384, :] + acc_ref[384:768, :]
    top, low = split2(source)
    place = place_ref[...]
    placed = dot(place, top) + dot(place, low)
    for i in range(3):
        for c in range(5):
            at = i * 200 + c * 40
            block = placed[at : at + 40, :] - div_ref[at : at + 40, :]
            for ex in range(EX):
                to = (i * 2 + ex) * 40
                z_ref[to : to + 40, c * 128 : (c + 1) * 128] = block[:, ex * 128 : (ex + 1) * 128]
    top, low = split2(z_ref[...])
    back = back_ref[...]
    nodal = dot(top, back) + dot(low, back)
    f_ref[...] = jnp.zeros_like(f_ref)
    for i in range(3):
        for ex in range(EX):
            for a in range(5):
                at = (i * 2 + ex) * 40 + a * 8
                for ey in range(EY):
                    to = (i * 9 + 4 * ex + a) * 24 + 4 * ey
                    f_ref[to : to + 8, :] += nodal[at : at + 8, ey * 128 : (ey + 1) * 128]
    for i in range(3):
        for x in range(9):
            at = (i * 9 + x) * 24
            if x < 8:
                main_out[i, x] = f_ref[at : at + 16, :]
            else:
                strike_out[i] = f_ref[at : at + 16, :]
            dip_out[i, x : x + 1, :] = f_ref[at + 16 : at + 17, :]


def source_forces(incoming, divergence):
    return pl.pallas_call(
        source_kernel,
        out_shape=[
            jax.ShapeDtypeStruct((3, 8, 16, 128), f32),
            jax.ShapeDtypeStruct((3, 9, 128), f32),
            jax.ShapeDtypeStruct((3, 16, 128), f32),
        ],
        scratch_shapes=[
            pltpu.VMEM((128, 128), f32),
            pltpu.VMEM((256, 128), f32),
            pltpu.VMEM((768, 1024), bf16),
            pltpu.VMEM((256, 1024), bf16),
            pltpu.VMEM((768, 256), f32),
            pltpu.VMEM((240, 640), f32),
            pltpu.VMEM((3 * 9 * 24, 128), f32),
        ],
        compiler_params=pltpu.CompilerParams(vmem_limit_bytes=LIMIT),
        cost_estimate=pl.CostEstimate(
            flops=7 * 10**9, bytes_accessed=2500000, transcendentals=0
        ),
        name="source_forces",
    )(incoming, divergence, jnp.asarray(PLACE, bf16), jnp.asarray(SELECT.T.copy(), bf16))


def update_kernel(
    disp_ref, veloc_ref, mass_ref, force_ref, dip_ref, strike_ref, disp_out, veloc_out, f_ref
):
    f_ref[...] = force_ref[...]
    for i in range(3):
        for x in range(8):
            f_ref[i, x, 0:1, :] += dip_ref[i, x : x + 1, :]
        f_ref[i, 0] += strike_ref[i]
    for i in range(3):
        veloc = veloc_ref[i] + time_step * (mass_ref[...] * f_ref[i])
        veloc_out[i] = veloc
        disp_out[i] = disp_ref[i] + time_step * veloc


def update(disp, veloc, mass, force, dip, strike):
    shape = jax.ShapeDtypeStruct((3, 8, 16, 128), f32)
    return pl.pallas_call(
        update_kernel,
        out_shape=[shape, shape],
        scratch_shapes=[pltpu.VMEM((3, 8, 16, 128), f32)],
        name="update",
    )(disp, veloc, mass, force, dip, strike)


def local(
    adj_disp,
    adj_veloc,
    fwd_disp,
    inv_mass,
    shear_mod,
    lame_mod,
    kernel_mu,
    kernel_kappa,
    chan_window,
    chan_dir,
    chan_local,
    chan_part,
    chan_elem,
):
    outgoing = pack(
        chan_window, chan_dir, chan_local, chan_part.reshape(1, NCH), chan_elem.reshape(1, NCH)
    )
    incoming = lax.all_to_all(
        outgoing.reshape(NDEV, 8, 128), ("gx", "gy"), split_axis=0, concat_axis=0, tiled=True
    )
    first = jnp.concatenate([adj_disp[:, 0], fwd_disp[:, 0]], axis=0)
    strike = shifted(first, "gx", -1)
    edge = jnp.concatenate([adj_disp[:, :, 0], fwd_disp[:, :, 0]], axis=0)
    dip = shifted(jnp.concatenate([edge, strike[:, 0:1]], axis=1), "gy", -1)
    mu_new, kappa_new, divergence = element_terms(
        adj_disp,
        fwd_disp,
        strike,
        dip,
        shear_mod.reshape(1, ELEMS),
        lame_mod.reshape(1, ELEMS),
        kernel_mu,
        kernel_kappa,
    )
    force, dip_force, strike_force = source_forces(incoming.reshape(NDEV * 8, 128), divergence)
    back_dip = shifted(dip_force, "gy", 1)
    back_strike = shifted(strike_force.at[:, 0].add(back_dip[:, 8]), "gx", 1)
    disp_new, veloc_new = update(adj_disp, adj_veloc, inv_mass, force, back_dip, back_strike)
    return (disp_new, veloc_new, mu_new, kappa_new)


def solution(mesh):
    return jax.shard_map(
        local,
        mesh=mesh,
        in_specs=(
            P(None, "gx", "gy", None),
            P(None, "gx", "gy", None),
            P(None, "gx", "gy", None),
            P("gx", "gy", None),
            P("gx", "gy", None),
            P("gx", "gy", None),
            P(None, ("gx", "gy")),
            P(None, ("gx", "gy")),
            P(None, ("gx", "gy")),
            P(None, ("gx", "gy")),
            P(None, ("gx", "gy")),
            P(("gx", "gy"), None),
            P(("gx", "gy")),
        ),
        out_specs=(
            P(None, "gx", "gy", None),
            P(None, "gx", "gy", None),
            P(None, ("gx", "gy")),
            P(None, ("gx", "gy")),
        ),
        check_vma=False,
    )
```

time: 637 us -> 82.2 us (0.13)
  the two profiles are of different devices: /device:TPU:1 before, /device:TPU:40 now
where the time goes in v1:
time: 82.2 us; the launch traced here: 81.6 us
  Pallas kernels  39 us (47%)
  starting transfers between devices  24.4 us (30%)
  waiting for transfers between devices  9.46 us (12%)
  local copies, waits for them, and re-layouts  7.24 us (9%)
    pallas_call x1, Pallas kernels, source_forces(): pl.pallas_call(source_kernel, out_shape=[jax.ShapeDtypeStruct((3, 8, 16,...  18.5 us
    ppermute x4, starting transfers between devices, shifted(): return lax.ppermute(x, axis, pairs)  14.3 us
    pallas_call x1, Pallas kernels, pack(): pl.pallas_call(pack_kernel, out_shape=jax.ShapeDtypeStruct((NDEV * 8, 128...  11.6 us
    all_to_all x1, starting transfers between devices, local(): lax.all_to_all(outgoing.reshape(NDEV, 8, 128), ('gx', 'gy'), split_axis=0...  10.1 us
    ppermute x4, waiting for transfers between devices, shifted(): return lax.ppermute(x, axis, pairs)  9.46 us
    pallas_call x1, Pallas kernels, element_terms(): pl.pallas_call(element_kernel, out_shape=[jax.ShapeDtypeStruct((125, ELEM...  6.9 us
    unnamed x14, local copies, waits for them, and re-layouts  2.04 us
    pallas_call x1, Pallas kernels, update(): pl.pallas_call(update_kernel, out_shape=[shape, shape], scratch_shapes=[p...  1.94 us
  transfers between devices with their start and end apart: 5, of which 3 were waited for; matrix products, arithmetic and copies ran while one was open for 4% of the time, Pallas kernels for 23%

profile of v1, /device:TPU:40, one launch (start us, length us, event | category | flops | bytes accessed | tf_op | source)
XLA Modules:
  0.0 81.6 jit_solution(15840486144321666673)
XLA Ops:
  0.6 0.8 slice_bitcast_fusion
  1.4 2.4 %collective-permute-start = (f32[6,16,128]{2,1,0:T(8,128)S(1)}, f32[6,16,128]{2,1,0:T(8,128)S(1)}, u32[]{:S(2)}, u32[]{:S(2)}) collective-permute-start(f32[6,16,128]{2,1,0:T(8,128)S(1)} %pad_maximum_fusion), channel_id=1, source_target_pairs={{8,0},{16,8},{24,16},{32,24},{40,32},{48,40},{56,48},{64,56},{72,6... | collective-permute-start | bytes 147464 | tf_op jit(solution)/shard_map/ppermute | solution.py:111
  3.8 11.6 %pack.1 = f32[1024,128]{1,0:T(8,128)} custom-call(f32[16,8192]{1,0:T(8,128)} %win_ref.1, f32[3,8192]{1,0:T(4,128)} %dir_ref.1, f32[3,8192]{1,0:T(4,128)} %loc_ref.1, s32[1,8192]{1,0:T(1,128)} %bitcast.22, s32[1,8192]{1,0:T(1,128)} %bitcast.23, f32[16,128]{1,0:T(8,128)} %constant.41.clone.coef_ref, bf16[256,384]{1,0:T(8,128)(2,1)} %constant.42.clone.upper_ref), custom_call_target="tpu_custom_call" | custom-call | flops 5000000000 | bytes 1500000 | tf_op jit(solution)/shard_map/pack/pallas_call | solution.py:180
  15.4 10.1 %all-to-all-start = ((f32[128,8,128]{2,1,0:T(8,128)}), f32[128,8,128]{2,1,0:T(8,128)S(1)}, u32[]{:S(2)}, u32[]{:S(2)}) async-start(f32[128,8,128]{2,1,0:T(8,128)} %bitcast.19), calls=%async_computation | async-start | bytes 1048576 | tf_op jit(solution)/shard_map/all_to_all | solution.py:484
  25.6 0.9 %slice.43 = f32[3,8,1,128]{3,2,1,0:T(1,128)S(1)} slice(f32[3,8,16,128]{3,2,1,0:T(8,128)} %fwd_ref.1), slice={[0:3], [0:8], [0:1], [0:128]} | slice | bytes 24576 | tf_op jit(solution)/shard_map/slice | solution.py:489
  26.5 0.9 %slice.42 = f32[3,8,1,128]{3,2,1,0:T(1,128)S(1)} slice(f32[3,8,16,128]{3,2,1,0:T(8,128)} %disp_ref.1), slice={[0:3], [0:8], [0:1], [0:128]} | slice | bytes 24576 | tf_op jit(solution)/shard_map/slice | solution.py:489
  27.4 0.0 collective-permute-done.strike_ref
  27.4 0.0 copy-start.5
  27.4 0.0 copy-start.3
  27.4 0.0 copy-start.4
  27.4 4.8 %collective-permute-start.1 = (f32[6,9,128]{2,1,0:T(8,128)S(1)}, f32[6,9,128]{2,1,0:T(8,128)S(1)}, u32[]{:S(2)}, u32[]{:S(2)}) collective-permute-start(f32[6,9,128]{2,1,0:T(8,128)S(1)} %pad_maximum_fusion.1), channel_id=1, source_target_pairs={{1,0},{2,1},{3,2},{4,3},{5,4},{6,5},{7,6},{9,8},{10,9},{11,10},{12... | collective-permute-start | bytes 82952 | tf_op jit(solution)/shard_map/ppermute | solution.py:111
  32.3 0.0 copy-done.3
  32.3 0.7 reshape.61.shear_ref
  32.9 0.0 copy-done.4
  33.0 0.7 reshape.62.lame_ref
  33.6 2.0 %collective-permute-done.1.dip_ref = f32[6,9,128]{2,1,0:T(8,128)S(1)} collective-permute-done((f32[6,9,128]{2,1,0:T(8,128)S(1)}, f32[6,9,128]{2,1,0:T(8,128)S(1)}, u32[]{:S(2)}, u32[]{:S(2)}) %collective-permute-start.1) | collective-permute-done | bytes 27680 | tf_op jit(solution)/shard_map/ppermute | solution.py:111
  35.6 0.0 copy-done.5
  35.6 0.0 copy-start.6
  35.6 0.6 copy-done.6
  36.2 6.9 %element_terms.1 = (f32[125,256]{1,0:T(8,128)}, f32[125,256]{1,0:T(8,128)}, f32[600,256]{1,0:T(8,128)}) custom-call(f32[3,8,16,128]{3,2,1,0:T(8,128)} %disp_ref.1, f32[3,8,16,128]{3,2,1,0:T(8,128)} %fwd_ref.1, f32[6,16,128]{2,1,0:T(8,128)} %copy-done.5, f32[6,9,128]{2,1,0:T(8,128)} %copy-done.6, f32[1,256]{1,0:T(1,128)} %reshape.61.shear_ref, ...), custom_call_target="tpu_custom_call" | custom-call | flops 5000000000 | bytes 5000000 | tf_op jit(solution)/shard_map/element_terms/pallas_call | solution.py:304
  43.1 0.0 all-to-all-done
  43.1 0.8 copy-done
  43.9 18.5 %source_forces.1 = (f32[3,8,16,128]{3,2,1,0:T(8,128)}, f32[3,9,128]{2,1,0:T(8,128)}, f32[3,16,128]{2,1,0:T(8,128)}) custom-call(f32[1024,128]{1,0:T(8,128)} %bitcast.18, f32[600,256]{1,0:T(8,128)} %get-tuple-element.24.div_ref, bf16[608,384]{1,0:T(8,128)(2,1)} %constant.46.clone.place_ref, bf16[640,512]{1,0:T(8,128)(2,1)} %constant.47.clone.back_ref), custom_call_target="tpu_custom_call" | custom-call | flops 7000000000 | bytes 2500000 | tf_op jit(solution)/shard_map/source_forces/pallas_call | solution.py:418
  62.4 5.1 %collective-permute-start.2 = (f32[3,9,128]{2,1,0:T(8,128)}, f32[3,9,128]{2,1,0:T(8,128)S(1)}, u32[]{:S(2)}, u32[]{:S(2)}) collective-permute-start(f32[3,9,128]{2,1,0:T(8,128)} %get-tuple-element.26), channel_id=1, source_target_pairs={{0,1},{1,2},{2,3},{3,4},{4,5},{5,6},{6,7},{8,9},{9,10},{10,11},{11... | collective-permute-start | bytes 41480 | tf_op jit(solution)/shard_map/ppermute | solution.py:111
  67.6 3.2 %collective-permute-done.2.dip_ref = f32[3,9,128]{2,1,0:T(8,128)S(1)} collective-permute-done((f32[3,9,128]{2,1,0:T(8,128)}, f32[3,9,128]{2,1,0:T(8,128)S(1)}, u32[]{:S(2)}, u32[]{:S(2)}) %collective-permute-start.2) | collective-permute-done | bytes 13856 | tf_op jit(solution)/shard_map/ppermute | solution.py:111
  70.7 0.7 slice_add_fusion
  71.5 1.3 %scatter-add.4 = f32[3,16,128]{2,1,0:T(8,128)} dynamic-update-slice(f32[3,16,128]{2,1,0:T(8,128)} %get-tuple-element.27, f32[3,1,128]{2,1,0:T(1,128)S(1)} %slice_add_fusion, s32[]{:T(128)} %constant.40.clone.1, s32[]{:T(128)} %constant.40.clone.1, s32[]{:T(128)} %constant.40.clone.1) | dynamic-update-slice | bytes 3076 | tf_op jit(solution)/shard_map/scatter-add | solution.py:503
  72.8 1.9 %collective-permute-start.3 = (f32[3,16,128]{2,1,0:T(8,128)}, f32[3,16,128]{2,1,0:T(8,128)S(1)}, u32[]{:S(2)}, u32[]{:S(2)}) collective-permute-start(f32[3,16,128]{2,1,0:T(8,128)} %scatter-add.4), channel_id=1, source_target_pairs={{0,8},{8,16},{16,24},{24,32},{32,40},{40,48},{48,56},{56,64},{64,7... | collective-permute-start | bytes 73736 | tf_op jit(solution)/shard_map/ppermute | solution.py:111
  74.7 4.3 %collective-permute-done.3.strike_ref = f32[3,16,128]{2,1,0:T(8,128)S(1)} collective-permute-done((f32[3,16,128]{2,1,0:T(8,128)}, f32[3,16,128]{2,1,0:T(8,128)S(1)}, u32[]{:S(2)}, u32[]{:S(2)}) %collective-permute-start.3) | collective-permute-done | bytes 24608 | tf_op jit(solution)/shard_map/ppermute | solution.py:111
  79.0 0.0 copy-done.1
  79.0 0.6 copy-done.2
  79.6 1.9 %update.1 = (f32[3,8,16,128]{3,2,1,0:T(8,128)}, f32[3,8,16,128]{3,2,1,0:T(8,128)}) custom-call(f32[3,8,16,128]{3,2,1,0:T(8,128)} %disp_ref.1, f32[3,8,16,128]{3,2,1,0:T(8,128)} %veloc_ref.1, f32[8,16,128]{2,1,0:T(8,128)} %mass_ref.1, f32[3,8,16,128]{3,2,1,0:T(8,128)} %get-tuple-element.25.force_ref, f32[3,9,128]{2,1,0:T(8,128)} %copy-done.1, ...), custom_call_target="tpu_custom_call" | custom-call | tf_op jit(solution)/shard_map/update/pallas_call | solution.py:458
  (6 shorter events, 0.0 us)
Async XLA Ops:
  1.4 26.0 %collective-permute-start = (f32[6,16,128]{2,1,0:T(8,128)S(1)}, f32[6,16,128]{2,1,0:T(8,128)S(1)}, u32[]{:S(2)}, u32[]{:S(2)}) collective-permute-start(f32[6,16,128]{2,1,0:T(8,128)S(1)} %pad_maximum_fusion), channel_id=1, source_target_pairs={{8,0},{16,8},{24,16},{32,24},{40,32},{48,40},{56,48},{64,56},{72,6... | collective-permute-start | bytes 147464 | tf_op jit(solution)/shard_map/ppermute | solution.py:111
  15.4 27.7 %all-to-all-start = ((f32[128,8,128]{2,1,0:T(8,128)}), f32[128,8,128]{2,1,0:T(8,128)S(1)}, u32[]{:S(2)}, u32[]{:S(2)}) async-start(f32[128,8,128]{2,1,0:T(8,128)} %bitcast.19), calls=%async_computation | async-start | bytes 1048576 | tf_op jit(solution)/shard_map/all_to_all | solution.py:484
  27.4 8.2 %copy-start.5 = (f32[6,16,128]{2,1,0:T(8,128)}, f32[6,16,128]{2,1,0:T(8,128)S(1)}, u32[]{:S(2)}) copy-start(f32[6,16,128]{2,1,0:T(8,128)S(1)} %collective-permute-done.strike_ref) | copy-start | bytes 147460
  27.4 4.9 %copy-start.3 = (f32[2,4,32]{2,1,0:T(4,128)S(1)}, f32[2,4,32]{2,1,0:T(4,128)}, u32[]{:S(2)}) copy-start(f32[2,4,32]{2,1,0:T(4,128)} %param.26) | copy-start | bytes 3076
  27.4 5.5 %copy-start.4 = (f32[2,4,32]{2,1,0:T(4,128)S(1)}, f32[2,4,32]{2,1,0:T(4,128)}, u32[]{:S(2)}) copy-start(f32[2,4,32]{2,1,0:T(4,128)} %param.27) | copy-start | bytes 3076
  27.4 8.1 %collective-permute-start.1 = (f32[6,9,128]{2,1,0:T(8,128)S(1)}, f32[6,9,128]{2,1,0:T(8,128)S(1)}, u32[]{:S(2)}, u32[]{:S(2)}) collective-permute-start(f32[6,9,128]{2,1,0:T(8,128)S(1)} %pad_maximum_fusion.1), channel_id=1, source_target_pairs={{1,0},{2,1},{3,2},{4,3},{5,4},{6,5},{7,6},{9,8},{10,9},{11,10},{12... | collective-permute-start | bytes 82952 | tf_op jit(solution)/shard_map/ppermute | solution.py:111
  35.6 0.6 copy-start.6
  43.1 0.8 copy-start
  62.4 8.3 %collective-permute-start.2 = (f32[3,9,128]{2,1,0:T(8,128)}, f32[3,9,128]{2,1,0:T(8,128)S(1)}, u32[]{:S(2)}, u32[]{:S(2)}) collective-permute-start(f32[3,9,128]{2,1,0:T(8,128)} %get-tuple-element.26), channel_id=1, source_target_pairs={{0,1},{1,2},{2,3},{3,4},{4,5},{5,6},{6,7},{8,9},{9,10},{10,11},{11... | collective-permute-start | bytes 41480 | tf_op jit(solution)/shard_map/ppermute | solution.py:111
  70.7 8.3 %copy-start.1 = (f32[3,9,128]{2,1,0:T(8,128)}, f32[3,9,128]{2,1,0:T(8,128)S(1)}, u32[]{:S(2)}) copy-start(f32[3,9,128]{2,1,0:T(8,128)S(1)} %collective-permute-done.2.dip_ref) | copy-start | bytes 41476
  72.8 6.2 %collective-permute-start.3 = (f32[3,16,128]{2,1,0:T(8,128)}, f32[3,16,128]{2,1,0:T(8,128)S(1)}, u32[]{:S(2)}, u32[]{:S(2)}) collective-permute-start(f32[3,16,128]{2,1,0:T(8,128)} %scatter-add.4), channel_id=1, source_target_pairs={{0,8},{8,16},{16,24},{24,32},{32,40},{40,48},{48,56},{56,64},{64,7... | collective-permute-start | bytes 73736 | tf_op jit(solution)/shard_map/ppermute | solution.py:111
  79.0 0.6 copy-start.2

commit v2 on v1

--- a/solution.py
+++ b/solution.py
@@ -16,6 +16,7 @@
 CAP = 128
 ELEMS = EX * EY * EZ
 LIMIT = 56 * 1024 * 1024
+LOW_LIMIT = 24 * 1024 * 1024
 
 
 def gll_tables():
@@ -96,19 +97,25 @@
                     bc = 5 * b + c
                     at = (i * 5 + a) * 24 + bc if bc < 24 else 360 + i * 5 + a
                     place[i * 200 + padded_row(c, a, b), at] = 1.0
-    upper = np.zeros((256, 384), np.float32)
-    upper[:, :256] = np.arange(256)[:, None] < np.arange(256)[None, :]
-    upper[:, 256:] = 1.0
+    upper = np.asarray(np.arange(256)[:, None] <= np.arange(256)[None, :], np.float32)
     return select, grad, div, place, upper
 
 
 SELECT, GRAD, DIV, PLACE, UPPER = build_tables()
 
 
-def shifted(x, axis, by):
-    peers = lax.axis_size(axis)
-    pairs = [(i, i + by) for i in range(peers) if 0 <= i + by < peers]
-    return lax.ppermute(x, axis, pairs)
+def shifted(x, step_x, step_y):
+    size_x, size_y = lax.axis_size("gx"), lax.axis_size("gy")
+    if step_y == 0:
+        return lax.ppermute(x, "gx", [(i, (i + step_x) % size_x) for i in range(size_x)])
+    if step_x == 0:
+        return lax.ppermute(x, "gy", [(i, (i + step_y) % size_y) for i in range(size_y)])
+    pairs = [
+        (i * size_y + j, (i + step_x) % size_x * size_y + (j + step_y) % size_y)
+        for i in range(size_x)
+        for j in range(size_y)
+    ]
+    return lax.ppermute(x, ("gx", "gy"), pairs)
 
 
 def dot(x, y):
@@ -124,29 +131,82 @@
     return top, (x - top.astype(f32)).astype(bf16)
 
 
-PACK_CHUNK = 512
+def low_row(row, rows):
+    tile = jnp.broadcast_to(row, (16, row.shape[1])).astype(bf16)
+    return jnp.concatenate([tile] * (rows // 16), axis=0)
+
+
+def one_hot(row, rows):
+    numbers = lax.broadcasted_iota(i32, (rows, row.shape[1]), 0).astype(f32).astype(bf16)
+    return jnp.where(numbers == low_row(row, rows), jnp.ones((), bf16), jnp.zeros((), bf16))
+
+
+PACK_CHUNK = 2048
+PACK_UNROLL = 2
 
 
 def pack_kernel(
-    win_ref, dir_ref, loc_ref, part_ref, elem_ref, coef_ref, upper_ref, out_ref, key_ref, a_ref, acc_ref
+    win_hbm,
+    dir_hbm,
+    loc_hbm,
+    part_hbm,
+    elem_hbm,
+    coef_hbm,
+    upper_hbm,
+    adj_hbm,
+    fwd_hbm,
+    out_ref,
+    edge_ref,
+    acc_ref,
+    win_ref,
+    dir_ref,
+    loc_ref,
+    part_ref,
+    elem_ref,
+    coef_ref,
+    upper_ref,
+    adj_ref,
+    fwd_ref,
+    sems,
+    *a_refs,
 ):
+    edge = pl.ds(0, 8)
+    pairs = [
+        (upper_hbm, upper_ref),
+        (part_hbm, part_ref),
+        (win_hbm, win_ref),
+        (coef_hbm, coef_ref),
+        (dir_hbm, dir_ref),
+        (loc_hbm, loc_ref),
+        (elem_hbm, elem_ref),
+        (adj_hbm.at[:, :, edge, :], adj_ref),
+        (fwd_hbm.at[:, :, edge, :], fwd_ref),
+    ]
+    copies = [pltpu.make_async_copy(a, b, sems.at[k]) for k, (a, b) in enumerate(pairs)]
+    for copy in copies:
+        copy.start()
+    acc_ref[...] = jnp.zeros_like(acc_ref)
+    for copy in copies[:7]:
+        copy.wait()
     upper = upper_ref[...]
-
-    def rank_step(at, base):
-        span = pl.ds(pl.multiple_of(at * 256, 256), 256)
-        target = part_ref[:, span]
-        same = lax.broadcasted_iota(i32, (NDEV, 256), 0) == target
-        running = dot(jnp.where(same, 1.0, 0.0).astype(bf16), upper)
-        before = running[:, :256] + jnp.concatenate([base, base], axis=1)
-        rank = jnp.sum(jnp.where(same, before, 0.0), axis=0, keepdims=True)
-        key_ref[:, span] = rank.astype(i32) + (target >> 6) * CAP
-        return base + running[:, 256:]
-
-    lax.fori_loop(0, NCH // 256, rank_step, jnp.zeros((NDEV, 128), f32), unroll=4)
-    acc_ref[...] = jnp.zeros_like(acc_ref)
     coef = coef_ref[:, 0:1]
 
-    def fill_step(at, carry):
+    def fill(at, base, a_ref):
+        blocks = PACK_CHUNK // 256
+        targets, same = [], []
+        for block in range(blocks):
+            span = pl.ds(pl.multiple_of(at * PACK_CHUNK + block * 256, 256), 256)
+            targets.append(part_ref[:, span])
+            same.append(lax.broadcasted_iota(i32, (NDEV, 256), 0) == targets[block])
+        hits = jnp.concatenate([jnp.where(hit, 1.0, 0.0).astype(bf16) for hit in same], axis=0)
+        running = dot(hits, upper)
+        keys = []
+        for block in range(blocks):
+            upto = running[block * NDEV : (block + 1) * NDEV, :]
+            rank = jnp.sum(jnp.where(same[block], upto + base, 0.0), axis=0, keepdims=True)
+            keys.append(rank + ((targets[block] >> 6) * CAP - 1).astype(f32))
+            base = base + upto[:, 255:256]
+        key = jnp.concatenate(keys, axis=1)
         span = pl.ds(pl.multiple_of(at * PACK_CHUNK, PACK_CHUNK), PACK_CHUNK)
         strength = jnp.sum(win_ref[:, span] * coef, axis=0, keepdims=True)
         force = strength * dir_ref[:, span]
@@ -157,14 +217,18 @@
         rows = [force[k : k + 1] for k in range(3)] + [where_at[k : k + 1] for k in range(3)]
         rows += [force_low[k : k + 1] for k in range(3)] + [where_low[k : k + 1] for k in range(3)]
         rows += [elem]
-        mask = lax.broadcasted_iota(i32, (64, PACK_CHUNK), 0) == (part_ref[:, span] & 63)
+        mask = one_hot((part_ref[:, span] & 63).astype(f32), 64)
         for k, row in enumerate(rows):
-            a_ref[k * 64 : (k + 1) * 64, :] = jnp.where(mask, row, 0.0).astype(bf16)
-        slot = lax.broadcasted_iota(i32, (256, PACK_CHUNK), 0) == key_ref[:, span]
-        acc_ref[...] += dot_nt(a_ref[...], jnp.where(slot, 1.0, 0.0).astype(bf16))
-        return carry
-
-    lax.fori_loop(0, NCH // PACK_CHUNK, fill_step, 0)
+            a_ref[k * 64 : (k + 1) * 64, :] = mask * low_row(row, 64)
+        acc_ref[...] += dot_nt(a_ref[...], one_hot(key, 256))
+        return base
+
+    def step(at, base):
+        for k in range(PACK_UNROLL):
+            base = fill(at * PACK_UNROLL + k, base, a_refs[k])
+        return base
+
+    lax.fori_loop(0, NCH // PACK_CHUNK // PACK_UNROLL, step, jnp.zeros((NDEV, 1), f32))
     for half in range(2):
         lanes = slice(half * 128, (half + 1) * 128)
         for v in range(6):
@@ -173,24 +237,54 @@
             )
         out_ref[pl.ds(half * 512 + 6, 64, stride=8), :] = acc_ref[12 * 64 : 13 * 64, lanes]
         out_ref[pl.ds(half * 512 + 7, 64, stride=8), :] = jnp.zeros((64, 128), f32)
-
-
-def pack(chan_window, chan_dir, chan_local, part_row, elem_row):
+    for copy in copies[7:]:
+        copy.wait()
+    for f in range(6):
+        source = adj_ref if f < 3 else fwd_ref
+        for x in range(8):
+            edge_ref[f, x : x + 1, :] = source[f % 3, x, 0:1, :]
+
+
+def pack(chan_window, chan_dir, chan_local, part_row, elem_row, adj, fwd):
     coef = np.tile(time_filter().astype(np.float32)[:, None], (1, 128))
+    hbm = pl.BlockSpec(memory_space=pl.ANY)
     return pl.pallas_call(
         pack_kernel,
-        out_shape=jax.ShapeDtypeStruct((NDEV * 8, 128), f32),
+        out_shape=[
+            jax.ShapeDtypeStruct((NDEV * 8, 128), f32),
+            jax.ShapeDtypeStruct((6, 8, 128), f32),
+        ],
+        in_specs=[hbm] * 9,
         scratch_shapes=[
+            pltpu.VMEM((13 * 64, 256), f32),
+            pltpu.VMEM((NSAMP, NCH), f32),
+            pltpu.VMEM((3, NCH), f32),
+            pltpu.VMEM((3, NCH), f32),
             pltpu.VMEM((1, NCH), i32),
-            pltpu.VMEM((13 * 64, PACK_CHUNK), bf16),
-            pltpu.VMEM((13 * 64, 256), f32),
-        ],
+            pltpu.VMEM((1, NCH), i32),
+            pltpu.VMEM((NSAMP, 128), f32),
+            pltpu.VMEM((256, 256), bf16),
+            pltpu.VMEM((3, 8, 8, 128), f32),
+            pltpu.VMEM((3, 8, 8, 128), f32),
+            pltpu.SemaphoreType.DMA((9,)),
+        ]
+        + [pltpu.VMEM((13 * 64, PACK_CHUNK), bf16)] * PACK_UNROLL,
         compiler_params=pltpu.CompilerParams(vmem_limit_bytes=LIMIT),
         cost_estimate=pl.CostEstimate(
             flops=5 * 10**9, bytes_accessed=1500000, transcendentals=0
         ),
         name="pack",
-    )(chan_window, chan_dir, chan_local, part_row, elem_row, jnp.asarray(coef), jnp.asarray(UPPER, bf16))
+    )(
+        chan_window,
+        chan_dir,
+        chan_local,
+        part_row,
+        elem_row,
+        jnp.asarray(coef),
+        jnp.asarray(UPPER, bf16),
+        adj,
+        fwd,
+    )
 
 
 def element_kernel(
@@ -214,16 +308,20 @@
     g_ref,
     t_ref,
 ):
+    in_x = lax.axis_index("gx") < lax.axis_size("gx") - 1
+    in_y = lax.axis_index("gy") < lax.axis_size("gy") - 1
     for f in range(6):
         source = adj_ref if f < 3 else fwd_ref
         for x in range(9):
             base = (f * 9 + x) * 24
+            inside = in_y
             if x < 8:
                 n_ref[base : base + 16, :] = source[f % 3, x]
             else:
-                n_ref[base : base + 16, :] = strike_ref[f]
+                n_ref[base : base + 16, :] = jnp.where(in_x, strike_ref[f], 0.0)
+                inside = in_x & in_y
             n_ref[base + 16 : base + 24, :] = jnp.zeros((8, 128), f32)
-            n_ref[base + 16 : base + 17, :] = dip_ref[f, x : x + 1, :]
+            n_ref[base + 16 : base + 17, :] = jnp.where(inside, dip_ref[f, x : x + 1, :], 0.0)
     for f in range(6):
         for ex in range(EX):
             for a in range(5):
@@ -249,8 +347,8 @@
     g_ref[...] = both[:384] + (both[384:] + dot(grad_ref[:384, :], low))
     for ex in range(EX):
         lanes = slice(ex * 128, (ex + 1) * 128)
-        shear = shear_ref[:, lanes]
-        lame = lame_ref[:, lanes]
+        shear = jnp.concatenate([shear_ref[ex, ey : ey + 1, :] for ey in range(EY)], axis=1)
+        lame = jnp.concatenate([lame_ref[ex, ey : ey + 1, :] for ey in range(EY)], axis=1)
         bulk = lame + 2.0 / 3.0 * shear
         for tile in range(16):
             rows = slice(tile * 8, tile * 8 + 8)
@@ -315,12 +413,16 @@
             pltpu.VMEM((384, 1536), f32),
             pltpu.VMEM((384, 768), f32),
         ],
-        compiler_params=pltpu.CompilerParams(vmem_limit_bytes=LIMIT),
+        compiler_params=pltpu.CompilerParams(vmem_limit_bytes=LOW_LIMIT),
         cost_estimate=pl.CostEstimate(
             flops=5 * 10**9, bytes_accessed=5000000, transcendentals=0
         ),
         name="element_terms",
     )(adj, fwd, strike, dip, shear, lame, mu, kappa, jnp.asarray(SELECT, bf16), jnp.asarray(grad), jnp.asarray(div))
+
+
+GROUP = 8
+SPREAD_UNROLL = 4
 
 
 def source_kernel(
@@ -331,14 +433,13 @@
     main_out,
     dip_out,
     strike_out,
-    gx_ref,
-    yz_ref,
-    a_ref,
-    b_ref,
+    corner_out,
     acc_ref,
     z_ref,
     f_ref,
+    *parts_refs,
 ):
+    turns = 128 // GROUP // SPREAD_UNROLL
     acc_ref[...] = jnp.zeros_like(acc_ref)
 
     def basis(points):
@@ -354,34 +455,48 @@
             result.append(value * float(scale))
         return result
 
+    def spread(at, gx_ref, yz_ref, a_ref, b_ref):
+        for sub in range(GROUP // 8):
+            base = pl.multiple_of(at * (GROUP * 8) + sub * 64, 64)
+            values = [inc_ref[pl.ds(base + v, 8, stride=8), :] for v in range(7)]
+            lx, ly, lz = basis(values[3]), basis(values[4]), basis(values[5])
+            for i in range(3):
+                for a in range(5):
+                    gx_ref[pl.ds(sub * 128 + i * 5 + a, 8, stride=16), :] = values[i] * lx[a]
+            gx_ref[pl.ds(sub * 128 + 15, 8, stride=16), :] = jnp.zeros((8, 128), f32)
+            for b in range(5):
+                for c in range(5):
+                    yz_ref[pl.ds(sub * 256 + b * 5 + c, 8, stride=32), :] = ly[b] * lz[c]
+            index = values[6]
+            for k in range(8):
+                s = sub * 8 + k
+                lanes = slice(s * 128, (s + 1) * 128)
+                b_ref[:, lanes] = one_hot(index[k : k + 1, :], ELEMS)
+                yz = yz_ref[s * 32 : s * 32 + 24, :]
+                last = yz_ref[s * 32 + 24 : s * 32 + 25, :]
+                for pair in range(8):
+                    row = s * 16 + 2 * pair
+                    parts = [gx_ref[row : row + 1, :] * yz]
+                    if pair < 7:
+                        parts += [gx_ref[row + 1 : row + 2, :] * yz]
+                    else:
+                        parts += [gx_ref[s * 16 : s * 16 + 16, :] * last, jnp.zeros((8, 128), f32)]
+                    top, low = split2(jnp.concatenate(parts, axis=0))
+                    a_ref[pair * 48 : pair * 48 + 48, lanes] = top
+                    a_ref[384 + pair * 48 : 384 + pair * 48 + 48, lanes] = low
+
+    def gather(gx_ref, yz_ref, a_ref, b_ref):
+        acc_ref[...] += dot_nt(a_ref[...], b_ref[...])
+
+    sets = [parts_refs[4 * k : 4 * k + 4] for k in range(SPREAD_UNROLL)]
+
     def step(at, carry):
-        base = pl.multiple_of(at * 64, 64)
-        values = [inc_ref[pl.ds(base + v, 8, stride=8), :] for v in range(7)]
-        lx, ly, lz = basis(values[3]), basis(values[4]), basis(values[5])
-        for i in range(3):
-            for a in range(5):
-                gx_ref[pl.ds(i * 5 + a, 8, stride=16), :] = values[i] * lx[a]
-        gx_ref[pl.ds(15, 8, stride=16), :] = jnp.zeros((8, 128), f32)
-        for b in range(5):
-            for c in range(5):
-                yz_ref[pl.ds(b * 5 + c, 8, stride=32), :] = ly[b] * lz[c]
-        index = values[6].astype(i32)
-        for s in range(8):
-            yz = yz_ref[s * 32 : s * 32 + 24, :]
-            parts = [gx_ref[s * 16 + k : s * 16 + k + 1, :] * yz for k in range(15)]
-            parts.append(gx_ref[s * 16 : s * 16 + 16, :] * yz_ref[s * 32 + 24 : s * 32 + 25, :])
-            parts.append(jnp.zeros((8, 128), f32))
-            whole = jnp.concatenate(parts, axis=0)
-            top, low = split2(whole)
-            lanes = slice(s * 128, (s + 1) * 128)
-            a_ref[0:384, lanes] = top
-            a_ref[384:768, lanes] = low
-            here = lax.broadcasted_iota(i32, (ELEMS, 128), 0) == index[s : s + 1, :]
-            b_ref[:, lanes] = jnp.where(here, 1.0, 0.0).astype(bf16)
-        acc_ref[...] += dot_nt(a_ref[...], b_ref[...])
+        for k in range(SPREAD_UNROLL):
+            spread(at * SPREAD_UNROLL + k, *sets[k])
+            gather(*sets[k])
         return carry
 
-    lax.fori_loop(0, 16, step, 0)
+    lax.fori_loop(0, turns, step, 0)
     source = acc_ref[0:384, :] + acc_ref[384:768, :]
     top, low = split2(source)
     place = place_ref[...]
@@ -409,9 +524,10 @@
             at = (i * 9 + x) * 24
             if x < 8:
                 main_out[i, x] = f_ref[at : at + 16, :]
+                dip_out[i, x : x + 1, :] = f_ref[at + 16 : at + 17, :]
             else:
                 strike_out[i] = f_ref[at : at + 16, :]
-            dip_out[i, x : x + 1, :] = f_ref[at + 16 : at + 17, :]
+                corner_out[i : i + 1, :] = f_ref[at + 16 : at + 17, :]
 
 
 def source_forces(incoming, divergence):
@@ -419,19 +535,23 @@
         source_kernel,
         out_shape=[
             jax.ShapeDtypeStruct((3, 8, 16, 128), f32),
-            jax.ShapeDtypeStruct((3, 9, 128), f32),
+            jax.ShapeDtypeStruct((3, 8, 128), f32),
             jax.ShapeDtypeStruct((3, 16, 128), f32),
+            jax.ShapeDtypeStruct((3, 128), f32),
         ],
         scratch_shapes=[
-            pltpu.VMEM((128, 128), f32),
-            pltpu.VMEM((256, 128), f32),
-            pltpu.VMEM((768, 1024), bf16),
-            pltpu.VMEM((256, 1024), bf16),
             pltpu.VMEM((768, 256), f32),
             pltpu.VMEM((240, 640), f32),
             pltpu.VMEM((3 * 9 * 24, 128), f32),
-        ],
-        compiler_params=pltpu.CompilerParams(vmem_limit_bytes=LIMIT),
+        ]
+        + [
+            pltpu.VMEM((GROUP * 16, 128), f32),
+            pltpu.VMEM((GROUP * 32, 128), f32),
+            pltpu.VMEM((768, GROUP * 128), bf16),
+            pltpu.VMEM((256, GROUP * 128), bf16),
+        ]
+        * SPREAD_UNROLL,
+        compiler_params=pltpu.CompilerParams(vmem_limit_bytes=LOW_LIMIT),
         cost_estimate=pl.CostEstimate(
             flops=7 * 10**9, bytes_accessed=2500000, transcendentals=0
         ),
@@ -440,27 +560,31 @@
 
 
 def update_kernel(
-    disp_ref, veloc_ref, mass_ref, force_ref, dip_ref, strike_ref, disp_out, veloc_out, f_ref
+    disp_ref, veloc_ref, mass_ref, force_ref, dip_ref, strike_ref, corner_ref, disp_out, veloc_out, f_ref
 ):
+    in_x = lax.axis_index("gx") > 0
+    in_y = lax.axis_index("gy") > 0
     f_ref[...] = force_ref[...]
     for i in range(3):
         for x in range(8):
-            f_ref[i, x, 0:1, :] += dip_ref[i, x : x + 1, :]
-        f_ref[i, 0] += strike_ref[i]
+            f_ref[i, x, 0:1, :] += jnp.where(in_y, dip_ref[i, x : x + 1, :], 0.0)
+        f_ref[i, 0] += jnp.where(in_x, strike_ref[i], 0.0)
+        f_ref[i, 0, 0:1, :] += jnp.where(in_x & in_y, corner_ref[i : i + 1, :], 0.0)
     for i in range(3):
         veloc = veloc_ref[i] + time_step * (mass_ref[...] * f_ref[i])
         veloc_out[i] = veloc
         disp_out[i] = disp_ref[i] + time_step * veloc
 
 
-def update(disp, veloc, mass, force, dip, strike):
+def update(disp, veloc, mass, force, dip, strike, corner):
     shape = jax.ShapeDtypeStruct((3, 8, 16, 128), f32)
     return pl.pallas_call(
         update_kernel,
         out_shape=[shape, shape],
         scratch_shapes=[pltpu.VMEM((3, 8, 16, 128), f32)],
+        compiler_params=pltpu.CompilerParams(vmem_limit_bytes=8 * 1024 * 1024),
         name="update",
-    )(disp, veloc, mass, force, dip, strike)
+    )(disp, veloc, mass, force, dip, strike, corner)
 
 
 def local(
@@ -478,30 +602,36 @@
     chan_part,
     chan_elem,
 ):
-    outgoing = pack(
-        chan_window, chan_dir, chan_local, chan_part.reshape(1, NCH), chan_elem.reshape(1, NCH)
+    first = jnp.concatenate([adj_disp[:, 0], fwd_disp[:, 0]], axis=0)
+    strike = shifted(first, -1, 0)
+    outgoing, edge = pack(
+        chan_window,
+        chan_dir,
+        chan_local,
+        chan_part.reshape(1, NCH),
+        chan_elem.reshape(1, NCH),
+        adj_disp,
+        fwd_disp,
     )
     incoming = lax.all_to_all(
         outgoing.reshape(NDEV, 8, 128), ("gx", "gy"), split_axis=0, concat_axis=0, tiled=True
     )
-    first = jnp.concatenate([adj_disp[:, 0], fwd_disp[:, 0]], axis=0)
-    strike = shifted(first, "gx", -1)
-    edge = jnp.concatenate([adj_disp[:, :, 0], fwd_disp[:, :, 0]], axis=0)
-    dip = shifted(jnp.concatenate([edge, strike[:, 0:1]], axis=1), "gy", -1)
+    dip = shifted(jnp.concatenate([edge, strike[:, 0:1]], axis=1), 0, -1)
     mu_new, kappa_new, divergence = element_terms(
+        adj_disp, fwd_disp, strike, dip, shear_mod, lame_mod, kernel_mu, kernel_kappa
+    )
+    force, dip_force, strike_force, corner_force = source_forces(
+        incoming.reshape(NDEV * 8, 128), divergence
+    )
+    disp_new, veloc_new = update(
         adj_disp,
-        fwd_disp,
-        strike,
-        dip,
-        shear_mod.reshape(1, ELEMS),
-        lame_mod.reshape(1, ELEMS),
-        kernel_mu,
-        kernel_kappa,
+        adj_veloc,
+        inv_mass,
+        force,
+        shifted(dip_force, 0, 1),
+        shifted(strike_force, 1, 0),
+        shifted(corner_force, 1, 1),
     )
-    force, dip_force, strike_force = source_forces(incoming.reshape(NDEV * 8, 128), divergence)
-    back_dip = shifted(dip_force, "gy", 1)
-    back_strike = shifted(strike_force.at[:, 0].add(back_dip[:, 8]), "gx", 1)
-    disp_new, veloc_new = update(adj_disp, adj_veloc, inv_mass, force, back_dip, back_strike)
     return (disp_new, veloc_new, mu_new, kappa_new)
 
 

time: 82.2 us -> 66.6 us (0.81)
  the two profiles are of different devices: /device:TPU:40 before, /device:TPU:1 now
where the time goes in v2:
time: 66.6 us; the launch traced here: 66.2 us
  Pallas kernels  29.1 us (44%)
  starting transfers between devices  22.1 us (33%)
  waiting for transfers between devices  9.66 us (15%)
  local copies, waits for them, and re-layouts  3.71 us (6%)
  between operations  0.83 us (1%)
  other arithmetic  0.76 us (1%)
    pallas_call x1, Pallas kernels, source_forces(): pl.pallas_call(source_kernel, out_shape=[jax.ShapeDtypeStruct((3, 8, 16,...  14.4 us
    all_to_all x1, starting transfers between devices, local(): lax.all_to_all(outgoing.reshape(NDEV, 8, 128), ('gx', 'gy'), split_axis=0...  10.7 us
    pallas_call x1, Pallas kernels, pack(): pl.pallas_call(pack_kernel, out_shape=[jax.ShapeDtypeStruct((NDEV * 8, 12...  9.46 us
    ppermute x2, starting transfers between devices, shifted(): lax.ppermute(x, 'gy', [(i, (i + step_y) % size_y) for i in range(size_y)])  7.84 us
    ppermute x1, waiting for transfers between devices, shifted(): return lax.ppermute(x, ('gx', 'gy'), pairs)  5.96 us
    pallas_call x1, Pallas kernels, element_terms(): pl.pallas_call(element_kernel, out_shape=[jax.ShapeDtypeStruct((125, ELEM...  4.46 us
    ppermute x2, waiting for transfers between devices, shifted(): lax.ppermute(x, 'gy', [(i, (i + step_y) % size_y) for i in range(size_y)])  3.7 us
    unnamed x30, local copies, waits for them, and re-layouts  2.94 us
  transfers between devices with their start and end apart: 6, of which 2 were waited for; matrix products, arithmetic and copies ran while one was open for 1% of the time, Pallas kernels for 21%

profile of v2, /device:TPU:1, one launch (start us, length us, event | category | flops | bytes accessed | tf_op | source)
XLA Modules:
  0.0 66.2 jit_solution(7398991198856585711)
XLA Ops:
  0.6 0.8 %slice_bitcast_fusion = (f32[3,16,128]{2,1,0:T(8,128)S(1)}, f32[3,16,128]{2,1,0:T(8,128)S(1)}) fusion(f32[3,8,16,128]{3,2,1,0:T(8,128)} %fwd_ref.1, f32[3,8,16,128]{3,2,1,0:T(8,128)} %disp_ref.1), kind=kLoop, calls=%fused_computation.2 | loop fusion | bytes 98304 | tf_op jit(solution)/shard_map/squeeze | solution.py:605
  1.4 1.5 %collective-permute-start = (f32[6,16,128]{2,1,0:T(8,128)S(1)}, f32[6,16,128]{2,1,0:T(8,128)S(1)}, u32[]{:S(2)}, u32[]{:S(2)}) collective-permute-start(f32[6,16,128]{2,1,0:T(8,128)S(1)} %pad_maximum_fusion), channel_id=1, source_target_pairs={{0,120},{8,0},{16,8},{24,16},{32,24},{40,32},{48,40},{56,48},{64,5... | collective-permute-start | bytes 147464 | tf_op jit(solution)/shard_map/ppermute | solution.py:110
  2.9 9.5 %pack.1 = (f32[1024,128]{1,0:T(8,128)}, f32[6,8,128]{2,1,0:T(8,128)}) custom-call(f32[16,8192]{1,0:T(8,128)} %win_hbm.1, f32[3,8192]{1,0:T(4,128)} %dir_hbm.1, f32[3,8192]{1,0:T(4,128)} %loc_hbm.1, s32[1,8192]{1,0:T(1,128)} %bitcast.14, s32[1,8192]{1,0:T(1,128)} %bitcast.15, f32[16,128]{1,0:T(8,128)} %constant.14.clone.coef_hbm, ...), custom_call_target="tpu_custom_call" | custom-call | flops 5000000000 | bytes 1500000 | tf_op jit(solution)/shard_map/pack/pallas_call | solution.py:251
  12.4 0.0 copy-start
  12.4 0.0 copy-start.3
  12.4 0.0 copy-start.4
  12.4 0.0 copy-start.5
  12.4 0.0 copy-start.11
  12.4 10.7 %all-to-all-start = ((f32[128,8,128]{2,1,0:T(8,128)}), f32[128,8,128]{2,1,0:T(8,128)S(1)}, u32[]{:S(2)}, u32[]{:S(2)}) async-start(f32[128,8,128]{2,1,0:T(8,128)} %bitcast.13), calls=%async_computation | async-start | bytes 1048576 | tf_op jit(solution)/shard_map/all_to_all | solution.py:616
  23.2 0.0 collective-permute-done.strike_ref
  23.2 0.0 copy-start.6
  23.2 0.0 copy-start.7
  23.2 0.8 %pad_maximum_fusion.1 = f32[6,9,128]{2,1,0:T(8,128)S(1)} fusion(f32[6,1,128]{2,1,0:T(1,128)S(1)} %slice.12, f32[6,8,128]{2,1,0:T(8,128)} %get-tuple-element.16), kind=kLoop, calls=%fused_computation.1 | loop fusion | flops 6912 | bytes 55296 | tf_op jit(solution)/shard_map/concatenate | solution.py:619
  24.0 5.2 %collective-permute-start.1 = (f32[6,9,128]{2,1,0:T(8,128)S(1)}, f32[6,9,128]{2,1,0:T(8,128)S(1)}, u32[]{:S(2)}, u32[]{:S(2)}) collective-permute-start(f32[6,9,128]{2,1,0:T(8,128)S(1)} %pad_maximum_fusion.1), channel_id=1, source_target_pairs={{0,7},{1,0},{2,1},{3,2},{4,3},{5,4},{6,5},{7,6},{8,15},{9,8},{10,9... | collective-permute-start | bytes 82952 | tf_op jit(solution)/shard_map/ppermute | solution.py:112
  29.1 3.7 %collective-permute-done.1.dip_ref = f32[6,9,128]{2,1,0:T(8,128)S(1)} collective-permute-done((f32[6,9,128]{2,1,0:T(8,128)S(1)}, f32[6,9,128]{2,1,0:T(8,128)S(1)}, u32[]{:S(2)}, u32[]{:S(2)}) %collective-permute-start.1) | collective-permute-done | bytes 27680 | tf_op jit(solution)/shard_map/ppermute | solution.py:112
  32.8 0.0 copy-done.9
  32.8 0.0 copy-done.3
  32.9 0.0 copy-start.12
  32.9 1.0 %copy-done.12 = bf16[416,384]{1,0:T(8,128)(2,1)S(1)} copy-done((bf16[416,384]{1,0:T(8,128)(2,1)S(1)}, bf16[416,384]{1,0:T(8,128)(2,1)}, u32[]{:S(2)}) %copy-start.12) | copy-done | bytes 319512
  33.8 4.5 %element_terms.1 = (f32[125,256]{1,0:T(8,128)}, f32[125,256]{1,0:T(8,128)}, f32[600,256]{1,0:T(8,128)S(1)}) custom-call(f32[3,8,16,128]{3,2,1,0:T(8,128)S(1)} %copy-done, f32[3,8,16,128]{3,2,1,0:T(8,128)S(1)} %copy-done.3, f32[6,16,128]{2,1,0:T(8,128)S(1)} %collective-permute-done.strike_ref, f32[6,9,128]{2,1,0:T(8,128)S(1)} %collective-permute-done.1.dip_ref, ...), custom_call_target="tpu_custom_call" | custom-call | flops 5000000000 | bytes 5000000 | tf_op jit(solution)/shard_map/element_terms/pallas_call | solution.py:402
  38.3 0.8 %copy-done.13 = f32[600,256]{1,0:T(8,128)} copy-done((f32[600,256]{1,0:T(8,128)}, f32[600,256]{1,0:T(8,128)S(1)}, u32[]{:S(2)}) %copy-start.13) | copy-done | bytes 614424
  39.2 0.0 all-to-all-done
  39.2 0.0 copy-done.8
  39.2 1.1 %copy-done.14 = f32[600,256]{1,0:T(8,128)S(1)} copy-done((f32[600,256]{1,0:T(8,128)S(1)}, f32[600,256]{1,0:T(8,128)}, u32[]{:S(2)}) %copy-start.14) | copy-done | bytes 614424
  40.3 14.4 %source_forces.1 = (f32[3,8,16,128]{3,2,1,0:T(8,128)S(1)}, f32[3,8,128]{2,1,0:T(8,128)S(1)}, f32[3,16,128]{2,1,0:T(8,128)S(1)}, f32[3,128]{1,0:T(4,128)S(1)}) custom-call(f32[1024,128]{1,0:T(8,128)S(1)} %bitcast.12, f32[600,256]{1,0:T(8,128)S(1)} %copy-done.14, bf16[608,384]{1,0:T(8,128)(2,1)S(1)} %copy-done.10, bf16[640,512]{1,0:T(8,128)(2,1)S(1)} %copy-done.8), custom_call_target="tpu_custom_call" | custom-call | flops 7000000000 | bytes 2500000 | tf_op jit(solution)/shard_map/source_forces/pallas_call | solution.py:534
  54.6 1.1 %collective-permute-start.3 = (f32[3,16,128]{2,1,0:T(8,128)S(1)}, f32[3,16,128]{2,1,0:T(8,128)S(1)}, u32[]{:S(2)}, u32[]{:S(2)}) collective-permute-start(f32[3,16,128]{2,1,0:T(8,128)S(1)} %get-tuple-element.20), channel_id=1, source_target_pairs={{0,8},{8,16},{16,24},{24,32},{32,40},{40,48},{48,56},{56,64},{64,7... | collective-permute-start | bytes 73736 | tf_op jit(solution)/shard_map/ppermute | solution.py:110
  55.8 2.7 %collective-permute-start.2 = (f32[3,8,128]{2,1,0:T(8,128)S(1)}, f32[3,8,128]{2,1,0:T(8,128)S(1)}, u32[]{:S(2)}, u32[]{:S(2)}) collective-permute-start(f32[3,8,128]{2,1,0:T(8,128)S(1)} %get-tuple-element.19), channel_id=1, source_target_pairs={{0,1},{1,2},{2,3},{3,4},{4,5},{5,6},{6,7},{7,0},{8,9},{9,10},{10,1... | collective-permute-start | bytes 36872 | tf_op jit(solution)/shard_map/ppermute | solution.py:112
  58.4 1.0 %collective-permute-start.4 = (f32[3,128]{1,0:T(4,128)S(1)}, f32[3,128]{1,0:T(4,128)S(1)}, u32[]{:S(2)}, u32[]{:S(2)}) collective-permute-start(f32[3,128]{1,0:T(4,128)S(1)} %get-tuple-element.21), channel_id=1, source_target_pairs={{0,9},{1,10},{2,11},{3,12},{4,13},{5,14},{6,15},{7,8},{8,17},{9,18... | collective-permute-start | bytes 4616 | tf_op jit(solution)/shard_map/ppermute | solution.py:118
  59.4 6.0 %collective-permute-done.4.corner_ref = f32[3,128]{1,0:T(4,128)S(1)} collective-permute-done((f32[3,128]{1,0:T(4,128)S(1)}, f32[3,128]{1,0:T(4,128)S(1)}, u32[]{:S(2)}, u32[]{:S(2)}) %collective-permute-start.4) | collective-permute-done | bytes 1568 | tf_op jit(solution)/shard_map/ppermute | solution.py:118
  65.4 0.0 collective-permute-done.2.dip_ref
  65.4 0.0 collective-permute-done.3.strike_ref
  65.4 0.8 %update.1 = (f32[3,8,16,128]{3,2,1,0:T(8,128)}, f32[3,8,16,128]{3,2,1,0:T(8,128)}) custom-call(f32[3,8,16,128]{3,2,1,0:T(8,128)S(1)} %copy-done, f32[3,8,16,128]{3,2,1,0:T(8,128)S(1)} %copy-done.1, f32[8,16,128]{2,1,0:T(8,128)S(1)} %copy-done.2, f32[3,8,16,128]{3,2,1,0:T(8,128)S(1)} %get-tuple-element.18.force_ref, ...), custom_call_target="tpu_custom_call" | custom-call | tf_op jit(solution)/shard_map/update/pallas_call | solution.py:581
  (18 shorter events, 0.0 us)
Async XLA Ops:
  1.4 21.8 %collective-permute-start = (f32[6,16,128]{2,1,0:T(8,128)S(1)}, f32[6,16,128]{2,1,0:T(8,128)S(1)}, u32[]{:S(2)}, u32[]{:S(2)}) collective-permute-start(f32[6,16,128]{2,1,0:T(8,128)S(1)} %pad_maximum_fusion), channel_id=1, source_target_pairs={{0,120},{8,0},{16,8},{24,16},{32,24},{40,32},{48,40},{56,48},{64,5... | collective-permute-start | bytes 147464 | tf_op jit(solution)/shard_map/ppermute | solution.py:110
  2.9 29.9 %copy-start.9 = (bf16[512,640]{1,0:T(8,128)(2,1)S(1)}, bf16[512,640]{1,0:T(8,128)(2,1)}, u32[]{:S(2)}) copy-start(bf16[512,640]{1,0:T(8,128)(2,1)} %constant.16.clone.select_ref) | copy-start | bytes 1966084
  12.4 20.5 %copy-start = (f32[3,8,16,128]{3,2,1,0:T(8,128)S(1)}, f32[3,8,16,128]{3,2,1,0:T(8,128)}, u32[]{:S(2)}) copy-start(f32[3,8,16,128]{3,2,1,0:T(8,128)} %disp_ref.1) | copy-start | bytes 589828
  12.4 20.4 %copy-start.3 = (f32[3,8,16,128]{3,2,1,0:T(8,128)S(1)}, f32[3,8,16,128]{3,2,1,0:T(8,128)}, u32[]{:S(2)}) copy-start(f32[3,8,16,128]{3,2,1,0:T(8,128)} %fwd_ref.1) | copy-start | bytes 589828
  12.4 20.4 %copy-start.4 = (f32[125,256]{1,0:T(8,128)S(1)}, f32[125,256]{1,0:T(8,128)}, u32[]{:S(2)}) copy-start(f32[125,256]{1,0:T(8,128)} %mu_ref.1) | copy-start | bytes 384004
  12.4 20.4 %copy-start.5 = (f32[125,256]{1,0:T(8,128)S(1)}, f32[125,256]{1,0:T(8,128)}, u32[]{:S(2)}) copy-start(f32[125,256]{1,0:T(8,128)} %kappa_ref.1) | copy-start | bytes 384004
  12.4 20.4 %copy-start.11 = (bf16[768,208]{1,0:T(8,128)(2,1)S(1)}, bf16[768,208]{1,0:T(8,128)(2,1)}, u32[]{:S(2)}) copy-start(bf16[768,208]{1,0:T(8,128)(2,1)} %constant.17.clone.grad_ref) | copy-start | bytes 958468
  12.4 26.7 %all-to-all-start = ((f32[128,8,128]{2,1,0:T(8,128)}), f32[128,8,128]{2,1,0:T(8,128)S(1)}, u32[]{:S(2)}, u32[]{:S(2)}) async-start(f32[128,8,128]{2,1,0:T(8,128)} %bitcast.13), calls=%async_computation | async-start | bytes 1048576 | tf_op jit(solution)/shard_map/all_to_all | solution.py:616
  23.2 9.7 %copy-start.6 = (f32[2,4,32]{2,1,0:T(4,128)S(1)}, f32[2,4,32]{2,1,0:T(4,128)}, u32[]{:S(2)}) copy-start(f32[2,4,32]{2,1,0:T(4,128)} %shear_ref.1) | copy-start | bytes 3076
  23.2 9.7 %copy-start.7 = (f32[2,4,32]{2,1,0:T(4,128)S(1)}, f32[2,4,32]{2,1,0:T(4,128)}, u32[]{:S(2)}) copy-start(f32[2,4,32]{2,1,0:T(4,128)} %lame_ref.1) | copy-start | bytes 3076
  24.0 15.2 %copy-start.8 = (bf16[640,512]{1,0:T(8,128)(2,1)S(1)}, bf16[640,512]{1,0:T(8,128)(2,1)}, u32[]{:S(2)}) copy-start(bf16[640,512]{1,0:T(8,128)(2,1)} %constant.20.clone.back_ref) | copy-start | bytes 1966084
  24.0 15.2 %copy-start.10 = (bf16[608,384]{1,0:T(8,128)(2,1)S(1)}, bf16[608,384]{1,0:T(8,128)(2,1)}, u32[]{:S(2)}) copy-start(bf16[608,384]{1,0:T(8,128)(2,1)} %constant.19.clone.place_ref) | copy-start | bytes 1400836
  24.0 8.8 %collective-permute-start.1 = (f32[6,9,128]{2,1,0:T(8,128)S(1)}, f32[6,9,128]{2,1,0:T(8,128)S(1)}, u32[]{:S(2)}, u32[]{:S(2)}) collective-permute-start(f32[6,9,128]{2,1,0:T(8,128)S(1)} %pad_maximum_fusion.1), channel_id=1, source_target_pairs={{0,7},{1,0},{2,1},{3,2},{4,3},{5,4},{6,5},{7,6},{8,15},{9,8},{10,9... | collective-permute-start | bytes 82952 | tf_op jit(solution)/shard_map/ppermute | solution.py:112
  32.9 1.0 %copy-start.12 = (bf16[416,384]{1,0:T(8,128)(2,1)S(1)}, bf16[416,384]{1,0:T(8,128)(2,1)}, u32[]{:S(2)}) copy-start(bf16[416,384]{1,0:T(8,128)(2,1)} %constant.18.clone.div_ref) | copy-start | bytes 958468
  38.3 0.9 %copy-start.13 = (f32[600,256]{1,0:T(8,128)}, f32[600,256]{1,0:T(8,128)S(1)}, u32[]{:S(2)}) copy-start(f32[600,256]{1,0:T(8,128)S(1)} %get-tuple-element.17.div_ref) | copy-start | bytes 1843204
  39.2 1.1 %copy-start.14 = (f32[600,256]{1,0:T(8,128)S(1)}, f32[600,256]{1,0:T(8,128)}, u32[]{:S(2)}) copy-start(f32[600,256]{1,0:T(8,128)} %copy-done.13) | copy-start | bytes 1843204
  40.3 25.1 %copy-start.1 = (f32[3,8,16,128]{3,2,1,0:T(8,128)S(1)}, f32[3,8,16,128]{3,2,1,0:T(8,128)}, u32[]{:S(2)}) copy-start(f32[3,8,16,128]{3,2,1,0:T(8,128)} %veloc_ref.1) | copy-start | bytes 589828
  40.3 25.1 %copy-start.2 = (f32[8,16,128]{2,1,0:T(8,128)S(1)}, f32[8,16,128]{2,1,0:T(8,128)}, u32[]{:S(2)}) copy-start(f32[8,16,128]{2,1,0:T(8,128)} %mass_ref.1) | copy-start | bytes 196612
  54.6 10.7 %collective-permute-start.3 = (f32[3,16,128]{2,1,0:T(8,128)S(1)}, f32[3,16,128]{2,1,0:T(8,128)S(1)}, u32[]{:S(2)}, u32[]{:S(2)}) collective-permute-start(f32[3,16,128]{2,1,0:T(8,128)S(1)} %get-tuple-element.20), channel_id=1, source_target_pairs={{0,8},{8,16},{16,24},{24,32},{32,40},{40,48},{48,56},{56,64},{64,7... | collective-permute-start | bytes 73736 | tf_op jit(solution)/shard_map/ppermute | solution.py:110
  55.8 9.6 %collective-permute-start.2 = (f32[3,8,128]{2,1,0:T(8,128)S(1)}, f32[3,8,128]{2,1,0:T(8,128)S(1)}, u32[]{:S(2)}, u32[]{:S(2)}) collective-permute-start(f32[3,8,128]{2,1,0:T(8,128)S(1)} %get-tuple-element.19), channel_id=1, source_target_pairs={{0,1},{1,2},{2,3},{3,4},{4,5},{5,6},{6,7},{7,0},{8,9},{9,10},{10,1... | collective-permute-start | bytes 36872 | tf_op jit(solution)/shard_map/ppermute | solution.py:112
  58.4 6.9 %collective-permute-start.4 = (f32[3,128]{1,0:T(4,128)S(1)}, f32[3,128]{1,0:T(4,128)S(1)}, u32[]{:S(2)}, u32[]{:S(2)}) collective-permute-start(f32[3,128]{1,0:T(4,128)S(1)} %get-tuple-element.21), channel_id=1, source_target_pairs={{0,9},{1,10},{2,11},{3,12},{4,13},{5,14},{6,15},{7,8},{8,17},{9,18... | collective-permute-start | bytes 4616 | tf_op jit(solution)/shard_map/ppermute | solution.py:118

commit v3 on v2

--- a/solution.py
+++ b/solution.py
@@ -70,7 +70,7 @@
                 if 4 * ez + c < 128:
                     select[ey * 128 + 4 * ez + c, c * 128 + ey * 32 + ez] = 1.0
     grad = np.zeros((384, 208))
-    div = np.zeros((208, 384))
+    div = np.zeros((128, 384))
     for a in range(5):
         for b in range(5):
             for c in range(5):
@@ -79,7 +79,8 @@
                     grad[row, padded_row(c, p, b)] += deriv[a, p]
                     grad[128 + row, padded_row(c, a, p)] += deriv[b, p]
                     grad[256 + row, padded_row(p, a, b)] += deriv[c, p]
-                    out = padded_row(c, a, b)
+                    bc = 5 * b + c
+                    out = a * 24 + bc if bc < 24 else 120 + a
                     div[out, 25 * p + 5 * b + c] += (
                         deriv[p, a] * weights[p] * weights[b] * weights[c]
                     )
@@ -287,6 +288,14 @@
     )
 
 
+def select_matrix():
+    lane = lax.broadcasted_iota(i32, (1, 640), 1)
+    at = 4 * (lane & 31) + (lane >> 7)
+    row = (lane >> 5) & 3
+    parts = [one_hot(jnp.where(row == ey, at, 255).astype(f32), 128) for ey in range(EY)]
+    return jnp.concatenate(parts, axis=0)
+
+
 def element_kernel(
     adj_ref,
     fwd_ref,
@@ -296,9 +305,7 @@
     lame_ref,
     mu_ref,
     kappa_ref,
-    select_ref,
-    grad_ref,
-    div_ref,
+    table_ref,
     mu_out,
     kappa_out,
     force_out,
@@ -334,7 +341,7 @@
     rest = whole - top.astype(f32)
     mid = rest.astype(bf16)
     low = (rest - mid.astype(f32)).astype(bf16)
-    select = select_ref[...]
+    select = select_matrix()
     opened = (dot(low, select) + dot(mid, select)) + dot(top, select)
     for block in range(12):
         for c in range(5):
@@ -343,8 +350,8 @@
             ]
     u_ref[200:208, :] = jnp.zeros((8, 1536), f32)
     top, low = split2(u_ref[...])
-    both = dot(grad_ref[...], top)
-    g_ref[...] = both[:384] + (both[384:] + dot(grad_ref[:384, :], low))
+    both = dot(table_ref[0:768, 0:208], top)
+    g_ref[...] = both[:384] + (both[384:] + dot(table_ref[0:384, 0:208], low))
     for ex in range(EX):
         lanes = slice(ex * 128, (ex + 1) * 128)
         shear = jnp.concatenate([shear_ref[ex, ey : ey + 1, :] for ey in range(EY)], axis=1)
@@ -390,21 +397,26 @@
             mu_out[rows, lanes] = mu_ref[rows, lanes] + (time_step * twice * product)[:count]
             kappa_out[rows, lanes] = kappa_ref[rows, lanes] + (time_step * bulk * traces)[:count]
     top, low = split2(t_ref[...])
-    both = dot(div_ref[...], top)
-    result = both[:208] + (both[208:] + dot(div_ref[:208, :], low))
+    both = dot(table_ref[768:1024, :], top)
+    result = both[:128] + (both[128:] + dot(table_ref[768:896, :], low))
     for i in range(3):
-        force_out[i * 200 : (i + 1) * 200, :] = result[:200, i * 256 : (i + 1) * 256]
+        lanes = slice(i * 256, (i + 1) * 256)
+        force_out[i * 120 : (i + 1) * 120, :] = result[:120, lanes]
+        force_out[360 + i * 5 : 365 + i * 5, :] = result[120:125, lanes]
+    force_out[375:384, :] = jnp.zeros((9, ELEMS), f32)
 
 
 def element_terms(adj, fwd, strike, dip, shear, lame, mu, kappa):
     grad = np.concatenate(halves(GRAD), axis=0)
-    div = np.concatenate(halves(DIV), axis=0)
+    table = np.zeros((1024, 384), grad.dtype)
+    table[:768, :208] = grad
+    table[768:] = np.concatenate(halves(DIV), axis=0)
     return pl.pallas_call(
         element_kernel,
         out_shape=[
             jax.ShapeDtypeStruct((125, ELEMS), f32),
             jax.ShapeDtypeStruct((125, ELEMS), f32),
-            jax.ShapeDtypeStruct((600, ELEMS), f32),
+            jax.ShapeDtypeStruct((384, ELEMS), f32),
         ],
         scratch_shapes=[
             pltpu.VMEM((6 * 9 * 24, 128), f32),
@@ -418,7 +430,7 @@
             flops=5 * 10**9, bytes_accessed=5000000, transcendentals=0
         ),
         name="element_terms",
-    )(adj, fwd, strike, dip, shear, lame, mu, kappa, jnp.asarray(SELECT, bf16), jnp.asarray(grad), jnp.asarray(div))
+    )(adj, fwd, strike, dip, shear, lame, mu, kappa, jnp.asarray(table))
 
 
 GROUP = 8
@@ -428,8 +440,7 @@
 def source_kernel(
     inc_ref,
     div_ref,
-    place_ref,
-    back_ref,
+    table_ref,
     main_out,
     dip_out,
     strike_out,
@@ -497,19 +508,19 @@
         return carry
 
     lax.fori_loop(0, turns, step, 0)
-    source = acc_ref[0:384, :] + acc_ref[384:768, :]
-    top, low = split2(source)
-    place = place_ref[...]
+    total = acc_ref[0:384, :] + acc_ref[384:768, :] - div_ref[...]
+    top, low = split2(total)
+    place = table_ref[0:608, 0:384]
     placed = dot(place, top) + dot(place, low)
     for i in range(3):
         for c in range(5):
             at = i * 200 + c * 40
-            block = placed[at : at + 40, :] - div_ref[at : at + 40, :]
+            block = placed[at : at + 40, :]
             for ex in range(EX):
                 to = (i * 2 + ex) * 40
                 z_ref[to : to + 40, c * 128 : (c + 1) * 128] = block[:, ex * 128 : (ex + 1) * 128]
     top, low = split2(z_ref[...])
-    back = back_ref[...]
+    back = table_ref[608:1248, :]
     nodal = dot(top, back) + dot(low, back)
     f_ref[...] = jnp.zeros_like(f_ref)
     for i in range(3):
@@ -531,6 +542,9 @@
 
 
 def source_forces(incoming, divergence):
+    table = np.zeros((1248, 512), np.float32)
+    table[:608, :384] = PLACE
+    table[608:] = SELECT.T
     return pl.pallas_call(
         source_kernel,
         out_shape=[
@@ -552,11 +566,8 @@
         ]
         * SPREAD_UNROLL,
         compiler_params=pltpu.CompilerParams(vmem_limit_bytes=LOW_LIMIT),
-        cost_estimate=pl.CostEstimate(
-            flops=7 * 10**9, bytes_accessed=2500000, transcendentals=0
-        ),
         name="source_forces",
-    )(incoming, divergence, jnp.asarray(PLACE, bf16), jnp.asarray(SELECT.T.copy(), bf16))
+    )(incoming, divergence, jnp.asarray(table, bf16))
 
 
 def update_kernel(

time: 66.6 us -> 64.4 us (0.967)
  local copies, waits for them, and re-layouts: 3.71 us -> 1.94 us
    unnamed x30 -> x20, local copies, waits for them, and re-layouts: 2.94 us -> 1.17 us
where the time goes in v3:
time: 64.4 us; the launch traced here: 64 us
  Pallas kernels  28.8 us (45%)
  starting transfers between devices  22.1 us (34%)
  waiting for transfers between devices  9.76 us (15%)
  local copies, waits for them, and re-layouts  1.94 us (3%)
  between operations  0.76 us (1%)
  other arithmetic  0.75 us (1%)
    pallas_call x1, Pallas kernels, source_forces(): pl.pallas_call(source_kernel, out_shape=[jax.ShapeDtypeStruct((3, 8, 16,...  14.4 us
    all_to_all x1, starting transfers between devices, local(): lax.all_to_all(outgoing.reshape(NDEV, 8, 128), ('gx', 'gy'), split_axis=0...  10.7 us
    pallas_call x1, Pallas kernels, pack(): pl.pallas_call(pack_kernel, out_shape=[jax.ShapeDtypeStruct((NDEV * 8, 12...  9.44 us
    ppermute x2, starting transfers between devices, shifted(): lax.ppermute(x, 'gy', [(i, (i + step_y) % size_y) for i in range(size_y)])  7.78 us
    ppermute x1, waiting for transfers between devices, shifted(): return lax.ppermute(x, ('gx', 'gy'), pairs)  5.95 us
    pallas_call x1, Pallas kernels, element_terms(): pl.pallas_call(element_kernel, out_shape=[jax.ShapeDtypeStruct((125, ELEM...  4.13 us
    ppermute x2, waiting for transfers between devices, shifted(): lax.ppermute(x, 'gy', [(i, (i + step_y) % size_y) for i in range(size_y)])  3.8 us
    ppermute x2, starting transfers between devices, shifted(): lax.ppermute(x, 'gx', [(i, (i + step_x) % size_x) for i in range(size_x)])  2.6 us
  transfers between devices with their start and end apart: 6, of which 2 were waited for; matrix products, arithmetic and copies ran while one was open for 1% of the time, Pallas kernels for 21%

profile of v3, /device:TPU:1, one launch (start us, length us, event | category | flops | bytes accessed | tf_op | source)
XLA Modules:
  0.0 64.0 jit_solution(15434622922297691599)
XLA Ops:
  0.6 0.8 %slice_bitcast_fusion = (f32[3,16,128]{2,1,0:T(8,128)S(1)}, f32[3,16,128]{2,1,0:T(8,128)S(1)}) fusion(f32[3,8,16,128]{3,2,1,0:T(8,128)} %fwd_ref.1, f32[3,8,16,128]{3,2,1,0:T(8,128)} %disp_ref.1), kind=kLoop, calls=%fused_computation.2 | loop fusion | bytes 98304 | tf_op jit(solution)/shard_map/squeeze | solution.py:616
  1.4 1.5 %collective-permute-start = (f32[6,16,128]{2,1,0:T(8,128)S(1)}, f32[6,16,128]{2,1,0:T(8,128)S(1)}, u32[]{:S(2)}, u32[]{:S(2)}) collective-permute-start(f32[6,16,128]{2,1,0:T(8,128)S(1)} %pad_maximum_fusion), channel_id=1, source_target_pairs={{0,120},{8,0},{16,8},{24,16},{32,24},{40,32},{48,40},{56,48},{64,5... | collective-permute-start | bytes 147464 | tf_op jit(solution)/shard_map/ppermute | solution.py:111
  2.9 0.0 copy-start.1
  2.9 0.0 copy-start.7
  2.9 0.0 copy-start.8
  2.9 9.4 %pack.1 = (f32[1024,128]{1,0:T(8,128)}, f32[6,8,128]{2,1,0:T(8,128)}) custom-call(f32[16,8192]{1,0:T(8,128)} %win_hbm.1, f32[3,8192]{1,0:T(4,128)} %dir_hbm.1, f32[3,8192]{1,0:T(4,128)} %loc_hbm.1, s32[1,8192]{1,0:T(1,128)} %bitcast.14, s32[1,8192]{1,0:T(1,128)} %bitcast.15, f32[16,128]{1,0:T(8,128)} %constant.8.clone.coef_hbm, ...), custom_call_target="tpu_custom_call" | custom-call | flops 5000000000 | bytes 1500000 | tf_op jit(solution)/shard_map/pack/pallas_call | solution.py:252
  12.4 10.7 %all-to-all-start = ((f32[128,8,128]{2,1,0:T(8,128)}), f32[128,8,128]{2,1,0:T(8,128)S(1)}, u32[]{:S(2)}, u32[]{:S(2)}) async-start(f32[128,8,128]{2,1,0:T(8,128)} %bitcast.13), calls=%async_computation | async-start | bytes 1048576 | tf_op jit(solution)/shard_map/all_to_all | solution.py:627
  23.1 0.0 collective-permute-done.strike_ref
  23.1 0.7 %pad_maximum_fusion.1 = f32[6,9,128]{2,1,0:T(8,128)S(1)} fusion(f32[6,1,128]{2,1,0:T(1,128)S(1)} %slice.12, f32[6,8,128]{2,1,0:T(8,128)} %get-tuple-element.16), kind=kLoop, calls=%fused_computation.1 | loop fusion | flops 6912 | bytes 55296 | tf_op jit(solution)/shard_map/concatenate | solution.py:630
  23.9 5.1 %collective-permute-start.1 = (f32[6,9,128]{2,1,0:T(8,128)S(1)}, f32[6,9,128]{2,1,0:T(8,128)S(1)}, u32[]{:S(2)}, u32[]{:S(2)}) collective-permute-start(f32[6,9,128]{2,1,0:T(8,128)S(1)} %pad_maximum_fusion.1), channel_id=1, source_target_pairs={{0,7},{1,0},{2,1},{3,2},{4,3},{5,4},{6,5},{7,6},{8,15},{9,8},{10,9... | collective-permute-start | bytes 82952 | tf_op jit(solution)/shard_map/ppermute | solution.py:113
  29.0 3.8 %collective-permute-done.1.dip_ref = f32[6,9,128]{2,1,0:T(8,128)S(1)} collective-permute-done((f32[6,9,128]{2,1,0:T(8,128)S(1)}, f32[6,9,128]{2,1,0:T(8,128)S(1)}, u32[]{:S(2)}, u32[]{:S(2)}) %collective-permute-start.1) | collective-permute-done | bytes 27680 | tf_op jit(solution)/shard_map/ppermute | solution.py:113
  32.8 0.0 copy-done.1
  32.8 0.0 copy-done.4
  32.8 0.0 copy-done.5
  32.8 0.0 copy-done.6
  32.8 0.0 copy-done.7
  32.8 0.0 copy-done.8
  32.8 0.0 copy-start.9
  32.8 1.1 %copy-done.9 = bf16[1024,384]{1,0:T(8,128)(2,1)S(1)} copy-done((bf16[1024,384]{1,0:T(8,128)(2,1)S(1)}, bf16[1024,384]{1,0:T(8,128)(2,1)}, u32[]{:S(2)}) %copy-start.9) | copy-done | bytes 786456
  33.9 4.1 %element_terms.1 = (f32[125,256]{1,0:T(8,128)}, f32[125,256]{1,0:T(8,128)}, f32[384,256]{1,0:T(8,128)S(1)}) custom-call(f32[3,8,16,128]{3,2,1,0:T(8,128)S(1)} %copy-done.1, f32[3,8,16,128]{3,2,1,0:T(8,128)S(1)} %copy-done.4, f32[6,16,128]{2,1,0:T(8,128)S(1)} %collective-permute-done.strike_ref, f32[6,9,128]{2,1,0:T(8,128)S(1)} %collective-permute-done.1.dip_ref, ...), custom_call_target="tpu_custom_call" | custom-call | flops 5000000000 | bytes 5000000 | tf_op jit(solution)/shard_map/element_terms/pallas_call | solution.py:414
  38.1 0.0 all-to-all-done
  38.1 0.0 copy-done
  38.1 14.4 %source_forces.1 = (f32[3,8,16,128]{3,2,1,0:T(8,128)S(1)}, f32[3,8,128]{2,1,0:T(8,128)S(1)}, f32[3,16,128]{2,1,0:T(8,128)S(1)}, f32[3,128]{1,0:T(4,128)S(1)}) custom-call(f32[1024,128]{1,0:T(8,128)S(1)} %bitcast.12, f32[384,256]{1,0:T(8,128)S(1)} %get-tuple-element.17.div_ref, bf16[1248,512]{1,0:T(8,128)(2,1)S(1)} %copy-done), custom_call_target="tpu_custom_call" | custom-call | tf_op jit(solution)/shard_map/source_forces/pallas_call | solution.py:548
  52.5 1.1 %collective-permute-start.3 = (f32[3,16,128]{2,1,0:T(8,128)S(1)}, f32[3,16,128]{2,1,0:T(8,128)S(1)}, u32[]{:S(2)}, u32[]{:S(2)}) collective-permute-start(f32[3,16,128]{2,1,0:T(8,128)S(1)} %get-tuple-element.20), channel_id=1, source_target_pairs={{0,8},{8,16},{16,24},{24,32},{32,40},{40,48},{48,56},{56,64},{64,7... | collective-permute-start | bytes 73736 | tf_op jit(solution)/shard_map/ppermute | solution.py:111
  53.6 2.7 %collective-permute-start.2 = (f32[3,8,128]{2,1,0:T(8,128)S(1)}, f32[3,8,128]{2,1,0:T(8,128)S(1)}, u32[]{:S(2)}, u32[]{:S(2)}) collective-permute-start(f32[3,8,128]{2,1,0:T(8,128)S(1)} %get-tuple-element.19), channel_id=1, source_target_pairs={{0,1},{1,2},{2,3},{3,4},{4,5},{5,6},{6,7},{7,0},{8,9},{9,10},{10,1... | collective-permute-start | bytes 36872 | tf_op jit(solution)/shard_map/ppermute | solution.py:113
  56.3 1.0 %collective-permute-start.4 = (f32[3,128]{1,0:T(4,128)S(1)}, f32[3,128]{1,0:T(4,128)S(1)}, u32[]{:S(2)}, u32[]{:S(2)}) collective-permute-start(f32[3,128]{1,0:T(4,128)S(1)} %get-tuple-element.21), channel_id=1, source_target_pairs={{0,9},{1,10},{2,11},{3,12},{4,13},{5,14},{6,15},{7,8},{8,17},{9,18... | collective-permute-start | bytes 4616 | tf_op jit(solution)/shard_map/ppermute | solution.py:119
  57.3 5.9 %collective-permute-done.4.corner_ref = f32[3,128]{1,0:T(4,128)S(1)} collective-permute-done((f32[3,128]{1,0:T(4,128)S(1)}, f32[3,128]{1,0:T(4,128)S(1)}, u32[]{:S(2)}, u32[]{:S(2)}) %collective-permute-start.4) | collective-permute-done | bytes 1568 | tf_op jit(solution)/shard_map/ppermute | solution.py:119
  63.2 0.0 collective-permute-done.2.dip_ref
  63.2 0.0 collective-permute-done.3.strike_ref
  63.2 0.0 copy-done.2
  63.2 0.0 copy-done.3
  63.2 0.8 %update.1 = (f32[3,8,16,128]{3,2,1,0:T(8,128)}, f32[3,8,16,128]{3,2,1,0:T(8,128)}) custom-call(f32[3,8,16,128]{3,2,1,0:T(8,128)S(1)} %copy-done.1, f32[3,8,16,128]{3,2,1,0:T(8,128)S(1)} %copy-done.2, f32[8,16,128]{2,1,0:T(8,128)S(1)} %copy-done.3, f32[3,8,16,128]{3,2,1,0:T(8,128)S(1)} %get-tuple-element.18.force_ref, ...), custom_call_target="tpu_custom_call" | custom-call | tf_op jit(solution)/shard_map/update/pallas_call | solution.py:592
  (8 shorter events, 0.0 us)
Async XLA Ops:
  1.4 21.7 %collective-permute-start = (f32[6,16,128]{2,1,0:T(8,128)S(1)}, f32[6,16,128]{2,1,0:T(8,128)S(1)}, u32[]{:S(2)}, u32[]{:S(2)}) collective-permute-start(f32[6,16,128]{2,1,0:T(8,128)S(1)} %pad_maximum_fusion), channel_id=1, source_target_pairs={{0,120},{8,0},{16,8},{24,16},{32,24},{40,32},{48,40},{56,48},{64,5... | collective-permute-start | bytes 147464 | tf_op jit(solution)/shard_map/ppermute | solution.py:111
  2.9 29.9 %copy-start.1 = (f32[3,8,16,128]{3,2,1,0:T(8,128)S(1)}, f32[3,8,16,128]{3,2,1,0:T(8,128)}, u32[]{:S(2)}) copy-start(f32[3,8,16,128]{3,2,1,0:T(8,128)} %disp_ref.1) | copy-start | bytes 589828
  2.9 29.9 %copy-start.4 = (f32[3,8,16,128]{3,2,1,0:T(8,128)S(1)}, f32[3,8,16,128]{3,2,1,0:T(8,128)}, u32[]{:S(2)}) copy-start(f32[3,8,16,128]{3,2,1,0:T(8,128)} %fwd_ref.1) | copy-start | bytes 589828
  2.9 29.9 %copy-start.5 = (f32[125,256]{1,0:T(8,128)S(1)}, f32[125,256]{1,0:T(8,128)}, u32[]{:S(2)}) copy-start(f32[125,256]{1,0:T(8,128)} %mu_ref.1) | copy-start | bytes 384004
  2.9 29.9 %copy-start.6 = (f32[125,256]{1,0:T(8,128)S(1)}, f32[125,256]{1,0:T(8,128)}, u32[]{:S(2)}) copy-start(f32[125,256]{1,0:T(8,128)} %kappa_ref.1) | copy-start | bytes 384004
  2.9 29.9 %copy-start.7 = (f32[2,4,32]{2,1,0:T(4,128)S(1)}, f32[2,4,32]{2,1,0:T(4,128)}, u32[]{:S(2)}) copy-start(f32[2,4,32]{2,1,0:T(4,128)} %shear_ref.1) | copy-start | bytes 3076
  2.9 29.9 %copy-start.8 = (f32[2,4,32]{2,1,0:T(4,128)S(1)}, f32[2,4,32]{2,1,0:T(4,128)}, u32[]{:S(2)}) copy-start(f32[2,4,32]{2,1,0:T(4,128)} %lame_ref.1) | copy-start | bytes 3076
  12.4 25.7 %all-to-all-start = ((f32[128,8,128]{2,1,0:T(8,128)}), f32[128,8,128]{2,1,0:T(8,128)S(1)}, u32[]{:S(2)}, u32[]{:S(2)}) async-start(f32[128,8,128]{2,1,0:T(8,128)} %bitcast.13), calls=%async_computation | async-start | bytes 1048576 | tf_op jit(solution)/shard_map/all_to_all | solution.py:627
  23.9 14.2 %copy-start = (bf16[1248,512]{1,0:T(8,128)(2,1)S(1)}, bf16[1248,512]{1,0:T(8,128)(2,1)}, u32[]{:S(2)}) copy-start(bf16[1248,512]{1,0:T(8,128)(2,1)} %constant.11.clone.table_ref) | copy-start | bytes 3833860
  23.9 8.9 %collective-permute-start.1 = (f32[6,9,128]{2,1,0:T(8,128)S(1)}, f32[6,9,128]{2,1,0:T(8,128)S(1)}, u32[]{:S(2)}, u32[]{:S(2)}) collective-permute-start(f32[6,9,128]{2,1,0:T(8,128)S(1)} %pad_maximum_fusion.1), channel_id=1, source_target_pairs={{0,7},{1,0},{2,1},{3,2},{4,3},{5,4},{6,5},{7,6},{8,15},{9,8},{10,9... | collective-permute-start | bytes 82952 | tf_op jit(solution)/shard_map/ppermute | solution.py:113
  32.8 1.1 %copy-start.9 = (bf16[1024,384]{1,0:T(8,128)(2,1)S(1)}, bf16[1024,384]{1,0:T(8,128)(2,1)}, u32[]{:S(2)}) copy-start(bf16[1024,384]{1,0:T(8,128)(2,1)} %constant.10.clone.table_ref) | copy-start | bytes 2359300
  38.1 25.1 %copy-start.2 = (f32[3,8,16,128]{3,2,1,0:T(8,128)S(1)}, f32[3,8,16,128]{3,2,1,0:T(8,128)}, u32[]{:S(2)}) copy-start(f32[3,8,16,128]{3,2,1,0:T(8,128)} %veloc_ref.1) | copy-start | bytes 589828
  38.1 25.2 %copy-start.3 = (f32[8,16,128]{2,1,0:T(8,128)S(1)}, f32[8,16,128]{2,1,0:T(8,128)}, u32[]{:S(2)}) copy-start(f32[8,16,128]{2,1,0:T(8,128)} %mass_ref.1) | copy-start | bytes 196612
  52.5 10.7 %collective-permute-start.3 = (f32[3,16,128]{2,1,0:T(8,128)S(1)}, f32[3,16,128]{2,1,0:T(8,128)S(1)}, u32[]{:S(2)}, u32[]{:S(2)}) collective-permute-start(f32[3,16,128]{2,1,0:T(8,128)S(1)} %get-tuple-element.20), channel_id=1, source_target_pairs={{0,8},{8,16},{16,24},{24,32},{32,40},{40,48},{48,56},{56,64},{64,7... | collective-permute-start | bytes 73736 | tf_op jit(solution)/shard_map/ppermute | solution.py:111
  53.6 9.6 %collective-permute-start.2 = (f32[3,8,128]{2,1,0:T(8,128)S(1)}, f32[3,8,128]{2,1,0:T(8,128)S(1)}, u32[]{:S(2)}, u32[]{:S(2)}) collective-permute-start(f32[3,8,128]{2,1,0:T(8,128)S(1)} %get-tuple-element.19), channel_id=1, source_target_pairs={{0,1},{1,2},{2,3},{3,4},{4,5},{5,6},{6,7},{7,0},{8,9},{9,10},{10,1... | collective-permute-start | bytes 36872 | tf_op jit(solution)/shard_map/ppermute | solution.py:113
  56.3 6.9 %collective-permute-start.4 = (f32[3,128]{1,0:T(4,128)S(1)}, f32[3,128]{1,0:T(4,128)S(1)}, u32[]{:S(2)}, u32[]{:S(2)}) collective-permute-start(f32[3,128]{1,0:T(4,128)S(1)} %get-tuple-element.21), channel_id=1, source_target_pairs={{0,9},{1,10},{2,11},{3,12},{4,13},{5,14},{6,15},{7,8},{8,17},{9,18... | collective-permute-start | bytes 4616 | tf_op jit(solution)/shard_map/ppermute | solution.py:119

commit v4 on v3

--- a/solution.py
+++ b/solution.py
@@ -434,7 +434,7 @@
 
 
 GROUP = 8
-SPREAD_UNROLL = 4
+SPREAD_UNROLL = 8
 
 
 def source_kernel(
@@ -538,7 +538,9 @@
                 dip_out[i, x : x + 1, :] = f_ref[at + 16 : at + 17, :]
             else:
                 strike_out[i] = f_ref[at : at + 16, :]
-                corner_out[i : i + 1, :] = f_ref[at + 16 : at + 17, :]
+                corner_out[i, 0:24, :] = f_ref[at : at + 24, :]
+                corner_out[i, 24:32, :] = jnp.zeros((8, 128), f32)
+                dip_out[i, 8:24, :] = jnp.zeros((16, 128), f32)
 
 
 def source_forces(incoming, divergence):
@@ -549,9 +551,9 @@
         source_kernel,
         out_shape=[
             jax.ShapeDtypeStruct((3, 8, 16, 128), f32),
-            jax.ShapeDtypeStruct((3, 8, 128), f32),
+            jax.ShapeDtypeStruct((3, 24, 128), f32),
             jax.ShapeDtypeStruct((3, 16, 128), f32),
-            jax.ShapeDtypeStruct((3, 128), f32),
+            jax.ShapeDtypeStruct((3, 32, 128), f32),
         ],
         scratch_shapes=[
             pltpu.VMEM((768, 256), f32),
@@ -565,7 +567,7 @@
             pltpu.VMEM((256, GROUP * 128), bf16),
         ]
         * SPREAD_UNROLL,
-        compiler_params=pltpu.CompilerParams(vmem_limit_bytes=LOW_LIMIT),
+        compiler_params=pltpu.CompilerParams(vmem_limit_bytes=32 * 1024 * 1024),
         name="source_forces",
     )(incoming, divergence, jnp.asarray(table, bf16))
 
@@ -580,7 +582,7 @@
         for x in range(8):
             f_ref[i, x, 0:1, :] += jnp.where(in_y, dip_ref[i, x : x + 1, :], 0.0)
         f_ref[i, 0] += jnp.where(in_x, strike_ref[i], 0.0)
-        f_ref[i, 0, 0:1, :] += jnp.where(in_x & in_y, corner_ref[i : i + 1, :], 0.0)
+        f_ref[i, 0, 0:1, :] += jnp.where(in_x & in_y, corner_ref[i, 16:17, :], 0.0)
     for i in range(3):
         veloc = veloc_ref[i] + time_step * (mass_ref[...] * f_ref[i])
         veloc_out[i] = veloc

time: 64.4 us -> 62.8 us (0.975)
  waiting for transfers between devices: 9.76 us -> 8.32 us
    ppermute x1, waiting for transfers between devices: 5.95 us -> 0.01 us  [shifted(): return lax.ppermute(x, ('gx', 'gy'), pairs)]
    ppermute x2, waiting for transfers between devices: 3.8 us -> 7.29 us  [shifted(): lax.ppermute(x, 'gy', [(i, (i + step_y) % size_y) for i in range(size_y)])]
    ppermute x1, starting transfers between devices: 0.97 us -> 2.62 us  [shifted(): return lax.ppermute(x, ('gx', 'gy'), pairs)]
    ppermute x2, starting transfers between devices: 7.78 us -> 6.31 us  [shifted(): lax.ppermute(x, 'gy', [(i, (i + step_y) % size_y) for i in range(size_y)])]
    ppermute x2, waiting for transfers between devices: 0.01 us -> 1.02 us  [shifted(): lax.ppermute(x, 'gx', [(i, (i + step_x) % size_x) for i in range(size_x)])]
  transfers between devices with their start and end apart: 6 -> 6, of which waited for: 2 -> 3; matrix products, arithmetic and copies ran while one was open for 1% -> 1% of each run, Pallas kernels for 21% -> 22%
where the time goes in v4:
time: 62.8 us; the launch traced here: 62.4 us
  Pallas kernels  28.5 us (45%)
  starting transfers between devices  22.1 us (35%)
  waiting for transfers between devices  8.32 us (13%)
  local copies, waits for them, and re-layouts  1.94 us (3%)
  other arithmetic  0.75 us (1%)
  between operations  0.75 us (1%)
    pallas_call x1, Pallas kernels, source_forces(): pl.pallas_call(source_kernel, out_shape=[jax.ShapeDtypeStruct((3, 8, 16,...  14.2 us
    all_to_all x1, starting transfers between devices, local(): lax.all_to_all(outgoing.reshape(NDEV, 8, 128), ('gx', 'gy'), split_axis=0...  10.7 us
    pallas_call x1, Pallas kernels, pack(): pl.pallas_call(pack_kernel, out_shape=[jax.ShapeDtypeStruct((NDEV * 8, 12...  9.44 us
    ppermute x2, waiting for transfers between devices, shifted(): lax.ppermute(x, 'gy', [(i, (i + step_y) % size_y) for i in range(size_y)])  7.29 us
    ppermute x2, starting transfers between devices, shifted(): lax.ppermute(x, 'gy', [(i, (i + step_y) % size_y) for i in range(size_y)])  6.31 us
    pallas_call x1, Pallas kernels, element_terms(): pl.pallas_call(element_kernel, out_shape=[jax.ShapeDtypeStruct((125, ELEM...  4.12 us
    ppermute x1, starting transfers between devices, shifted(): return lax.ppermute(x, ('gx', 'gy'), pairs)  2.62 us
    ppermute x2, starting transfers between devices, shifted(): lax.ppermute(x, 'gx', [(i, (i + step_x) % size_x) for i in range(size_x)])  2.47 us
  transfers between devices with their start and end apart: 6, of which 3 were waited for; matrix products, arithmetic and copies ran while one was open for 1% of the time, Pallas kernels for 22%

profile of v4, /device:TPU:1, one launch (start us, length us, event | category | flops | bytes accessed | tf_op | source)
XLA Modules:
  0.0 62.4 jit_solution(6527339952811839687)
XLA Ops:
  0.6 0.8 %slice_bitcast_fusion = (f32[3,16,128]{2,1,0:T(8,128)S(1)}, f32[3,16,128]{2,1,0:T(8,128)S(1)}) fusion(f32[3,8,16,128]{3,2,1,0:T(8,128)} %fwd_ref.1, f32[3,8,16,128]{3,2,1,0:T(8,128)} %disp_ref.1), kind=kLoop, calls=%fused_computation.2 | loop fusion | bytes 98304 | tf_op jit(solution)/shard_map/squeeze | solution.py:618
  1.4 1.5 %collective-permute-start = (f32[6,16,128]{2,1,0:T(8,128)S(1)}, f32[6,16,128]{2,1,0:T(8,128)S(1)}, u32[]{:S(2)}, u32[]{:S(2)}) collective-permute-start(f32[6,16,128]{2,1,0:T(8,128)S(1)} %pad_maximum_fusion), channel_id=1, source_target_pairs={{0,120},{8,0},{16,8},{24,16},{32,24},{40,32},{48,40},{56,48},{64,5... | collective-permute-start | bytes 147464 | tf_op jit(solution)/shard_map/ppermute | solution.py:111
  2.9 0.0 copy-start.1
  2.9 0.0 copy-start.7
  2.9 0.0 copy-start.8
  2.9 9.4 %pack.1 = (f32[1024,128]{1,0:T(8,128)}, f32[6,8,128]{2,1,0:T(8,128)}) custom-call(f32[16,8192]{1,0:T(8,128)} %win_hbm.1, f32[3,8192]{1,0:T(4,128)} %dir_hbm.1, f32[3,8192]{1,0:T(4,128)} %loc_hbm.1, s32[1,8192]{1,0:T(1,128)} %bitcast.14, s32[1,8192]{1,0:T(1,128)} %bitcast.15, f32[16,128]{1,0:T(8,128)} %constant.8.clone.coef_hbm, ...), custom_call_target="tpu_custom_call" | custom-call | flops 5000000000 | bytes 1500000 | tf_op jit(solution)/shard_map/pack/pallas_call | solution.py:252
  12.4 10.7 %all-to-all-start = ((f32[128,8,128]{2,1,0:T(8,128)}), f32[128,8,128]{2,1,0:T(8,128)S(1)}, u32[]{:S(2)}, u32[]{:S(2)}) async-start(f32[128,8,128]{2,1,0:T(8,128)} %bitcast.13), calls=%async_computation | async-start | bytes 1048576 | tf_op jit(solution)/shard_map/all_to_all | solution.py:629
  23.1 0.0 collective-permute-done.strike_ref
  23.1 0.7 %pad_maximum_fusion.1 = f32[6,9,128]{2,1,0:T(8,128)S(1)} fusion(f32[6,1,128]{2,1,0:T(1,128)S(1)} %slice.12, f32[6,8,128]{2,1,0:T(8,128)} %get-tuple-element.16), kind=kLoop, calls=%fused_computation.1 | loop fusion | flops 6912 | bytes 55296 | tf_op jit(solution)/shard_map/concatenate | solution.py:632
  23.9 5.1 %collective-permute-start.1 = (f32[6,9,128]{2,1,0:T(8,128)S(1)}, f32[6,9,128]{2,1,0:T(8,128)S(1)}, u32[]{:S(2)}, u32[]{:S(2)}) collective-permute-start(f32[6,9,128]{2,1,0:T(8,128)S(1)} %pad_maximum_fusion.1), channel_id=1, source_target_pairs={{0,7},{1,0},{2,1},{3,2},{4,3},{5,4},{6,5},{7,6},{8,15},{9,8},{10,9... | collective-permute-start | bytes 82952 | tf_op jit(solution)/shard_map/ppermute | solution.py:113
  29.0 3.8 %collective-permute-done.1.dip_ref = f32[6,9,128]{2,1,0:T(8,128)S(1)} collective-permute-done((f32[6,9,128]{2,1,0:T(8,128)S(1)}, f32[6,9,128]{2,1,0:T(8,128)S(1)}, u32[]{:S(2)}, u32[]{:S(2)}) %collective-permute-start.1) | collective-permute-done | bytes 27680 | tf_op jit(solution)/shard_map/ppermute | solution.py:113
  32.8 0.0 copy-done.1
  32.8 0.0 copy-done.4
  32.8 0.0 copy-done.5
  32.8 0.0 copy-done.6
  32.8 0.0 copy-done.7
  32.8 0.0 copy-done.8
  32.8 0.0 copy-start.9
  32.8 1.1 %copy-done.9 = bf16[1024,384]{1,0:T(8,128)(2,1)S(1)} copy-done((bf16[1024,384]{1,0:T(8,128)(2,1)S(1)}, bf16[1024,384]{1,0:T(8,128)(2,1)}, u32[]{:S(2)}) %copy-start.9) | copy-done | bytes 786456
  33.9 4.1 %element_terms.1 = (f32[125,256]{1,0:T(8,128)}, f32[125,256]{1,0:T(8,128)}, f32[384,256]{1,0:T(8,128)S(1)}) custom-call(f32[3,8,16,128]{3,2,1,0:T(8,128)S(1)} %copy-done.1, f32[3,8,16,128]{3,2,1,0:T(8,128)S(1)} %copy-done.4, f32[6,16,128]{2,1,0:T(8,128)S(1)} %collective-permute-done.strike_ref, f32[6,9,128]{2,1,0:T(8,128)S(1)} %collective-permute-done.1.dip_ref, ...), custom_call_target="tpu_custom_call" | custom-call | flops 5000000000 | bytes 5000000 | tf_op jit(solution)/shard_map/element_terms/pallas_call | solution.py:414
  38.1 0.0 all-to-all-done
  38.1 0.0 copy-done
  38.1 14.2 %source_forces.1 = (f32[3,8,16,128]{3,2,1,0:T(8,128)S(1)}, f32[3,24,128]{2,1,0:T(8,128)S(1)}, f32[3,16,128]{2,1,0:T(8,128)S(1)}, f32[3,32,128]{2,1,0:T(8,128)S(1)}) custom-call(f32[1024,128]{1,0:T(8,128)S(1)} %bitcast.12, f32[384,256]{1,0:T(8,128)S(1)} %get-tuple-element.17.div_ref, bf16[1248,512]{1,0:T(8,128)(2,1)S(1)} %copy-done), custom_call_target="tpu_custom_call" | custom-call | tf_op jit(solution)/shard_map/source_forces/pallas_call | solution.py:550
  52.3 2.6 %collective-permute-start.4 = (f32[3,32,128]{2,1,0:T(8,128)S(1)}, f32[3,32,128]{2,1,0:T(8,128)S(1)}, u32[]{:S(2)}, u32[]{:S(2)}) collective-permute-start(f32[3,32,128]{2,1,0:T(8,128)S(1)} %get-tuple-element.21), channel_id=1, source_target_pairs={{0,9},{1,10},{2,11},{3,12},{4,13},{5,14},{6,15},{7,8},{8,17},{9,18... | collective-permute-start | bytes 147464 | tf_op jit(solution)/shard_map/ppermute | solution.py:119
  54.9 1.2 %collective-permute-start.2 = (f32[3,24,128]{2,1,0:T(8,128)S(1)}, f32[3,24,128]{2,1,0:T(8,128)S(1)}, u32[]{:S(2)}, u32[]{:S(2)}) collective-permute-start(f32[3,24,128]{2,1,0:T(8,128)S(1)} %get-tuple-element.19), channel_id=1, source_target_pairs={{0,1},{1,2},{2,3},{3,4},{4,5},{5,6},{6,7},{7,0},{8,9},{9,10},{10,1... | collective-permute-start | bytes 110600 | tf_op jit(solution)/shard_map/ppermute | solution.py:113
  56.1 1.0 %collective-permute-start.3 = (f32[3,16,128]{2,1,0:T(8,128)S(1)}, f32[3,16,128]{2,1,0:T(8,128)S(1)}, u32[]{:S(2)}, u32[]{:S(2)}) collective-permute-start(f32[3,16,128]{2,1,0:T(8,128)S(1)} %get-tuple-element.20), channel_id=1, source_target_pairs={{0,8},{8,16},{16,24},{24,32},{32,40},{40,48},{48,56},{56,64},{64,7... | collective-permute-start | bytes 73736 | tf_op jit(solution)/shard_map/ppermute | solution.py:111
  57.0 1.0 %collective-permute-done.3.strike_ref = f32[3,16,128]{2,1,0:T(8,128)S(1)} collective-permute-done((f32[3,16,128]{2,1,0:T(8,128)S(1)}, f32[3,16,128]{2,1,0:T(8,128)S(1)}, u32[]{:S(2)}, u32[]{:S(2)}) %collective-permute-start.3) | collective-permute-done | bytes 24608 | tf_op jit(solution)/shard_map/ppermute | solution.py:111
  58.1 3.5 %collective-permute-done.2.dip_ref = f32[3,24,128]{2,1,0:T(8,128)S(1)} collective-permute-done((f32[3,24,128]{2,1,0:T(8,128)S(1)}, f32[3,24,128]{2,1,0:T(8,128)S(1)}, u32[]{:S(2)}, u32[]{:S(2)}) %collective-permute-start.2) | collective-permute-done | bytes 36896 | tf_op jit(solution)/shard_map/ppermute | solution.py:113
  61.6 0.0 collective-permute-done.4.corner_ref
  61.6 0.0 copy-done.2
  61.6 0.0 copy-done.3
  61.6 0.8 %update.1 = (f32[3,8,16,128]{3,2,1,0:T(8,128)}, f32[3,8,16,128]{3,2,1,0:T(8,128)}) custom-call(f32[3,8,16,128]{3,2,1,0:T(8,128)S(1)} %copy-done.1, f32[3,8,16,128]{3,2,1,0:T(8,128)S(1)} %copy-done.2, f32[8,16,128]{2,1,0:T(8,128)S(1)} %copy-done.3, f32[3,8,16,128]{3,2,1,0:T(8,128)S(1)} %get-tuple-element.18.force_ref, ...), custom_call_target="tpu_custom_call" | custom-call | tf_op jit(solution)/shard_map/update/pallas_call | solution.py:594
  (8 shorter events, 0.0 us)
Async XLA Ops:
  1.4 21.7 %collective-permute-start = (f32[6,16,128]{2,1,0:T(8,128)S(1)}, f32[6,16,128]{2,1,0:T(8,128)S(1)}, u32[]{:S(2)}, u32[]{:S(2)}) collective-permute-start(f32[6,16,128]{2,1,0:T(8,128)S(1)} %pad_maximum_fusion), channel_id=1, source_target_pairs={{0,120},{8,0},{16,8},{24,16},{32,24},{40,32},{48,40},{56,48},{64,5... | collective-permute-start | bytes 147464 | tf_op jit(solution)/shard_map/ppermute | solution.py:111
  2.9 29.9 %copy-start.1 = (f32[3,8,16,128]{3,2,1,0:T(8,128)S(1)}, f32[3,8,16,128]{3,2,1,0:T(8,128)}, u32[]{:S(2)}) copy-start(f32[3,8,16,128]{3,2,1,0:T(8,128)} %disp_ref.1) | copy-start | bytes 589828
  2.9 29.9 %copy-start.4 = (f32[3,8,16,128]{3,2,1,0:T(8,128)S(1)}, f32[3,8,16,128]{3,2,1,0:T(8,128)}, u32[]{:S(2)}) copy-start(f32[3,8,16,128]{3,2,1,0:T(8,128)} %fwd_ref.1) | copy-start | bytes 589828
  2.9 29.9 %copy-start.5 = (f32[125,256]{1,0:T(8,128)S(1)}, f32[125,256]{1,0:T(8,128)}, u32[]{:S(2)}) copy-start(f32[125,256]{1,0:T(8,128)} %mu_ref.1) | copy-start | bytes 384004
  2.9 29.9 %copy-start.6 = (f32[125,256]{1,0:T(8,128)S(1)}, f32[125,256]{1,0:T(8,128)}, u32[]{:S(2)}) copy-start(f32[125,256]{1,0:T(8,128)} %kappa_ref.1) | copy-start | bytes 384004
  2.9 29.9 %copy-start.7 = (f32[2,4,32]{2,1,0:T(4,128)S(1)}, f32[2,4,32]{2,1,0:T(4,128)}, u32[]{:S(2)}) copy-start(f32[2,4,32]{2,1,0:T(4,128)} %shear_ref.1) | copy-start | bytes 3076
  2.9 29.9 %copy-start.8 = (f32[2,4,32]{2,1,0:T(4,128)S(1)}, f32[2,4,32]{2,1,0:T(4,128)}, u32[]{:S(2)}) copy-start(f32[2,4,32]{2,1,0:T(4,128)} %lame_ref.1) | copy-start | bytes 3076
  12.4 25.7 %all-to-all-start = ((f32[128,8,128]{2,1,0:T(8,128)}), f32[128,8,128]{2,1,0:T(8,128)S(1)}, u32[]{:S(2)}, u32[]{:S(2)}) async-start(f32[128,8,128]{2,1,0:T(8,128)} %bitcast.13), calls=%async_computation | async-start | bytes 1048576 | tf_op jit(solution)/shard_map/all_to_all | solution.py:629
  23.9 14.2 %copy-start = (bf16[1248,512]{1,0:T(8,128)(2,1)S(1)}, bf16[1248,512]{1,0:T(8,128)(2,1)}, u32[]{:S(2)}) copy-start(bf16[1248,512]{1,0:T(8,128)(2,1)} %constant.11.clone.table_ref) | copy-start | bytes 3833860
  23.9 8.9 %collective-permute-start.1 = (f32[6,9,128]{2,1,0:T(8,128)S(1)}, f32[6,9,128]{2,1,0:T(8,128)S(1)}, u32[]{:S(2)}, u32[]{:S(2)}) collective-permute-start(f32[6,9,128]{2,1,0:T(8,128)S(1)} %pad_maximum_fusion.1), channel_id=1, source_target_pairs={{0,7},{1,0},{2,1},{3,2},{4,3},{5,4},{6,5},{7,6},{8,15},{9,8},{10,9... | collective-permute-start | bytes 82952 | tf_op jit(solution)/shard_map/ppermute | solution.py:113
  32.8 1.1 %copy-start.9 = (bf16[1024,384]{1,0:T(8,128)(2,1)S(1)}, bf16[1024,384]{1,0:T(8,128)(2,1)}, u32[]{:S(2)}) copy-start(bf16[1024,384]{1,0:T(8,128)(2,1)} %constant.10.clone.table_ref) | copy-start | bytes 2359300
  38.1 23.5 %copy-start.2 = (f32[3,8,16,128]{3,2,1,0:T(8,128)S(1)}, f32[3,8,16,128]{3,2,1,0:T(8,128)}, u32[]{:S(2)}) copy-start(f32[3,8,16,128]{3,2,1,0:T(8,128)} %veloc_ref.1) | copy-start | bytes 589828
  38.1 23.5 %copy-start.3 = (f32[8,16,128]{2,1,0:T(8,128)S(1)}, f32[8,16,128]{2,1,0:T(8,128)}, u32[]{:S(2)}) copy-start(f32[8,16,128]{2,1,0:T(8,128)} %mass_ref.1) | copy-start | bytes 196612
  52.3 9.3 %collective-permute-start.4 = (f32[3,32,128]{2,1,0:T(8,128)S(1)}, f32[3,32,128]{2,1,0:T(8,128)S(1)}, u32[]{:S(2)}, u32[]{:S(2)}) collective-permute-start(f32[3,32,128]{2,1,0:T(8,128)S(1)} %get-tuple-element.21), channel_id=1, source_target_pairs={{0,9},{1,10},{2,11},{3,12},{4,13},{5,14},{6,15},{7,8},{8,17},{9,18... | collective-permute-start | bytes 147464 | tf_op jit(solution)/shard_map/ppermute | solution.py:119
  54.9 6.7 %collective-permute-start.2 = (f32[3,24,128]{2,1,0:T(8,128)S(1)}, f32[3,24,128]{2,1,0:T(8,128)S(1)}, u32[]{:S(2)}, u32[]{:S(2)}) collective-permute-start(f32[3,24,128]{2,1,0:T(8,128)S(1)} %get-tuple-element.19), channel_id=1, source_target_pairs={{0,1},{1,2},{2,3},{3,4},{4,5},{5,6},{6,7},{7,0},{8,9},{9,10},{10,1... | collective-permute-start | bytes 110600 | tf_op jit(solution)/shard_map/ppermute | solution.py:113
  56.1 2.0 %collective-permute-start.3 = (f32[3,16,128]{2,1,0:T(8,128)S(1)}, f32[3,16,128]{2,1,0:T(8,128)S(1)}, u32[]{:S(2)}, u32[]{:S(2)}) collective-permute-start(f32[3,16,128]{2,1,0:T(8,128)S(1)} %get-tuple-element.20), channel_id=1, source_target_pairs={{0,8},{8,16},{16,24},{24,32},{32,40},{40,48},{48,56},{56,64},{64,7... | collective-permute-start | bytes 73736 | tf_op jit(solution)/shard_map/ppermute | solution.py:111

commit v5 on v4

--- a/solution.py
+++ b/solution.py
@@ -350,7 +350,7 @@
             ]
     u_ref[200:208, :] = jnp.zeros((8, 1536), f32)
     top, low = split2(u_ref[...])
-    both = dot(table_ref[0:768, 0:208], top)
+    both = dot(table_ref[:, 0:208], top)
     g_ref[...] = both[:384] + (both[384:] + dot(table_ref[0:384, 0:208], low))
     for ex in range(EX):
         lanes = slice(ex * 128, (ex + 1) * 128)
@@ -397,8 +397,12 @@
             mu_out[rows, lanes] = mu_ref[rows, lanes] + (time_step * twice * product)[:count]
             kappa_out[rows, lanes] = kappa_ref[rows, lanes] + (time_step * bulk * traces)[:count]
     top, low = split2(t_ref[...])
-    both = dot(table_ref[768:1024, :], top)
-    result = both[:128] + (both[128:] + dot(table_ref[768:896, :], low))
+    result = jnp.zeros((128, 768), f32)
+    for j in range(3):
+        rows = slice(j * 128, (j + 1) * 128)
+        both = dot(table_ref[j * 256 : (j + 1) * 256, 256:384], top[rows])
+        rest = dot(table_ref[j * 256 : j * 256 + 128, 256:384], low[rows])
+        result = result + (both[:128] + (both[128:] + rest))
     for i in range(3):
         lanes = slice(i * 256, (i + 1) * 256)
         force_out[i * 120 : (i + 1) * 120, :] = result[:120, lanes]
@@ -408,9 +412,11 @@
 
 def element_terms(adj, fwd, strike, dip, shear, lame, mu, kappa):
     grad = np.concatenate(halves(GRAD), axis=0)
-    table = np.zeros((1024, 384), grad.dtype)
-    table[:768, :208] = grad
-    table[768:] = np.concatenate(halves(DIV), axis=0)
+    table = np.zeros((768, 384), grad.dtype)
+    table[:, :208] = grad
+    for j in range(3):
+        block = DIV[:, j * 128 : (j + 1) * 128]
+        table[j * 256 : (j + 1) * 256, 256:] = np.concatenate(halves(block), axis=0)
     return pl.pallas_call(
         element_kernel,
         out_shape=[

time: 62.8 us -> 62 us (0.987)
  local copies, waits for them, and re-layouts: 1.94 us -> 0.82 us
    unnamed x20, local copies, waits for them, and re-layouts: 1.17 us -> 0.05 us
  transfers between devices with their start and end apart: 6 -> 6, of which waited for: 3 -> 4; matrix products, arithmetic and copies ran while one was open for 1% -> 1% of each run, Pallas kernels for 22% -> 23%
where the time goes in v5:
time: 62 us; the launch traced here: 61.7 us
  Pallas kernels  28.9 us (47%)
  starting transfers between devices  22 us (35%)
  waiting for transfers between devices  8.51 us (14%)
  local copies, waits for them, and re-layouts  0.82 us (1%)
  between operations  0.77 us (1%)
  other arithmetic  0.75 us (1%)
    pallas_call x1, Pallas kernels, source_forces(): pl.pallas_call(source_kernel, out_shape=[jax.ShapeDtypeStruct((3, 8, 16,...  14.2 us
    all_to_all x1, starting transfers between devices, local(): lax.all_to_all(outgoing.reshape(NDEV, 8, 128), ('gx', 'gy'), split_axis=0...  10.7 us
    pallas_call x1, Pallas kernels, pack(): pl.pallas_call(pack_kernel, out_shape=[jax.ShapeDtypeStruct((NDEV * 8, 12...  9.47 us
    ppermute x2, waiting for transfers between devices, shifted(): lax.ppermute(x, 'gy', [(i, (i + step_y) % size_y) for i in range(size_y)])  7.29 us
    ppermute x2, starting transfers between devices, shifted(): lax.ppermute(x, 'gy', [(i, (i + step_y) % size_y) for i in range(size_y)])  6.3 us
    pallas_call x1, Pallas kernels, element_terms(): pl.pallas_call(element_kernel, out_shape=[jax.ShapeDtypeStruct((125, ELEM...  4.43 us
    ppermute x2, starting transfers between devices, shifted(): lax.ppermute(x, 'gx', [(i, (i + step_x) % size_x) for i in range(size_x)])  2.48 us
    ppermute x1, starting transfers between devices, shifted(): return lax.ppermute(x, ('gx', 'gy'), pairs)  2.45 us
  transfers between devices with their start and end apart: 6, of which 4 were waited for; matrix products, arithmetic and copies ran while one was open for 1% of the time, Pallas kernels for 23%

profile of v5, /device:TPU:1, one launch (start us, length us, event | category | flops | bytes accessed | tf_op | source)
XLA Modules:
  0.0 61.7 jit_solution(15905274782634464483)
XLA Ops:
  0.6 0.8 %slice_bitcast_fusion = (f32[3,16,128]{2,1,0:T(8,128)S(1)}, f32[3,16,128]{2,1,0:T(8,128)S(1)}) fusion(f32[3,8,16,128]{3,2,1,0:T(8,128)} %fwd_ref.1, f32[3,8,16,128]{3,2,1,0:T(8,128)} %disp_ref.1), kind=kLoop, calls=%fused_computation.2 | loop fusion | bytes 98304 | tf_op jit(solution)/shard_map/squeeze | solution.py:624
  1.4 1.5 %collective-permute-start = (f32[6,16,128]{2,1,0:T(8,128)S(1)}, f32[6,16,128]{2,1,0:T(8,128)S(1)}, u32[]{:S(2)}, u32[]{:S(2)}) collective-permute-start(f32[6,16,128]{2,1,0:T(8,128)S(1)} %pad_maximum_fusion), channel_id=1, source_target_pairs={{0,120},{8,0},{16,8},{24,16},{32,24},{40,32},{48,40},{56,48},{64,5... | collective-permute-start | bytes 147464 | tf_op jit(solution)/shard_map/ppermute | solution.py:111
  2.9 0.0 copy-start.7
  2.9 0.0 copy-start.8
  2.9 0.0 copy-start.9
  2.9 9.5 %pack.1 = (f32[1024,128]{1,0:T(8,128)}, f32[6,8,128]{2,1,0:T(8,128)}) custom-call(f32[16,8192]{1,0:T(8,128)} %win_hbm.1, f32[3,8192]{1,0:T(4,128)} %dir_hbm.1, f32[3,8192]{1,0:T(4,128)} %loc_hbm.1, s32[1,8192]{1,0:T(1,128)} %bitcast.14, s32[1,8192]{1,0:T(1,128)} %bitcast.15, f32[16,128]{1,0:T(8,128)} %constant.8.clone.coef_hbm, ...), custom_call_target="tpu_custom_call" | custom-call | flops 5000000000 | bytes 1500000 | tf_op jit(solution)/shard_map/pack/pallas_call | solution.py:252
  12.4 10.7 %all-to-all-start = ((f32[128,8,128]{2,1,0:T(8,128)}), f32[128,8,128]{2,1,0:T(8,128)S(1)}, u32[]{:S(2)}, u32[]{:S(2)}) async-start(f32[128,8,128]{2,1,0:T(8,128)} %bitcast.13), calls=%async_computation | async-start | bytes 1048576 | tf_op jit(solution)/shard_map/all_to_all | solution.py:635
  23.1 0.0 collective-permute-done.strike_ref
  23.2 0.7 %pad_maximum_fusion.1 = f32[6,9,128]{2,1,0:T(8,128)S(1)} fusion(f32[6,1,128]{2,1,0:T(1,128)S(1)} %slice.12, f32[6,8,128]{2,1,0:T(8,128)} %get-tuple-element.16), kind=kLoop, calls=%fused_computation.1 | loop fusion | flops 6912 | bytes 55296 | tf_op jit(solution)/shard_map/concatenate | solution.py:638
  23.9 5.1 %collective-permute-start.1 = (f32[6,9,128]{2,1,0:T(8,128)S(1)}, f32[6,9,128]{2,1,0:T(8,128)S(1)}, u32[]{:S(2)}, u32[]{:S(2)}) collective-permute-start(f32[6,9,128]{2,1,0:T(8,128)S(1)} %pad_maximum_fusion.1), channel_id=1, source_target_pairs={{0,7},{1,0},{2,1},{3,2},{4,3},{5,4},{6,5},{7,6},{8,15},{9,8},{10,9... | collective-permute-start | bytes 82952 | tf_op jit(solution)/shard_map/ppermute | solution.py:113
  29.0 3.8 %collective-permute-done.1.dip_ref = f32[6,9,128]{2,1,0:T(8,128)S(1)} collective-permute-done((f32[6,9,128]{2,1,0:T(8,128)S(1)}, f32[6,9,128]{2,1,0:T(8,128)S(1)}, u32[]{:S(2)}, u32[]{:S(2)}) %collective-permute-start.1) | collective-permute-done | bytes 27680 | tf_op jit(solution)/shard_map/ppermute | solution.py:113
  32.8 0.0 copy-done.1
  32.8 0.0 copy-done.4
  32.8 0.0 copy-done.5
  32.8 0.0 copy-done.6
  32.8 0.0 copy-done.7
  32.8 0.0 copy-done.8
  32.8 0.0 copy-done.9
  32.9 4.4 %element_terms.1 = (f32[125,256]{1,0:T(8,128)}, f32[125,256]{1,0:T(8,128)}, f32[384,256]{1,0:T(8,128)S(1)}) custom-call(f32[3,8,16,128]{3,2,1,0:T(8,128)S(1)} %copy-done.1, f32[3,8,16,128]{3,2,1,0:T(8,128)S(1)} %copy-done.4, f32[6,16,128]{2,1,0:T(8,128)S(1)} %collective-permute-done.strike_ref, f32[6,9,128]{2,1,0:T(8,128)S(1)} %collective-permute-done.1.dip_ref, ...), custom_call_target="tpu_custom_call" | custom-call | flops 5000000000 | bytes 5000000 | tf_op jit(solution)/shard_map/element_terms/pallas_call | solution.py:420
  37.3 0.0 copy-start.2
  37.3 0.0 copy-start.3
  37.3 0.2 all-to-all-done
  37.5 0.0 copy-done
  37.5 14.2 %source_forces.1 = (f32[3,8,16,128]{3,2,1,0:T(8,128)S(1)}, f32[3,24,128]{2,1,0:T(8,128)S(1)}, f32[3,16,128]{2,1,0:T(8,128)S(1)}, f32[3,32,128]{2,1,0:T(8,128)S(1)}) custom-call(f32[1024,128]{1,0:T(8,128)S(1)} %bitcast.12, f32[384,256]{1,0:T(8,128)S(1)} %get-tuple-element.17.div_ref, bf16[1248,512]{1,0:T(8,128)(2,1)S(1)} %copy-done), custom_call_target="tpu_custom_call" | custom-call | tf_op jit(solution)/shard_map/source_forces/pallas_call | solution.py:556
  51.7 2.5 %collective-permute-start.4 = (f32[3,32,128]{2,1,0:T(8,128)S(1)}, f32[3,32,128]{2,1,0:T(8,128)S(1)}, u32[]{:S(2)}, u32[]{:S(2)}) collective-permute-start(f32[3,32,128]{2,1,0:T(8,128)S(1)} %get-tuple-element.21), channel_id=1, source_target_pairs={{0,9},{1,10},{2,11},{3,12},{4,13},{5,14},{6,15},{7,8},{8,17},{9,18... | collective-permute-start | bytes 147464 | tf_op jit(solution)/shard_map/ppermute | solution.py:119
  54.1 1.2 %collective-permute-start.2 = (f32[3,24,128]{2,1,0:T(8,128)S(1)}, f32[3,24,128]{2,1,0:T(8,128)S(1)}, u32[]{:S(2)}, u32[]{:S(2)}) collective-permute-start(f32[3,24,128]{2,1,0:T(8,128)S(1)} %get-tuple-element.19), channel_id=1, source_target_pairs={{0,1},{1,2},{2,3},{3,4},{4,5},{5,6},{6,7},{7,0},{8,9},{9,10},{10,1... | collective-permute-start | bytes 110600 | tf_op jit(solution)/shard_map/ppermute | solution.py:113
  55.3 1.0 %collective-permute-start.3 = (f32[3,16,128]{2,1,0:T(8,128)S(1)}, f32[3,16,128]{2,1,0:T(8,128)S(1)}, u32[]{:S(2)}, u32[]{:S(2)}) collective-permute-start(f32[3,16,128]{2,1,0:T(8,128)S(1)} %get-tuple-element.20), channel_id=1, source_target_pairs={{0,8},{8,16},{16,24},{24,32},{32,40},{40,48},{48,56},{56,64},{64,7... | collective-permute-start | bytes 73736 | tf_op jit(solution)/shard_map/ppermute | solution.py:111
  56.3 1.0 %collective-permute-done.3.strike_ref = f32[3,16,128]{2,1,0:T(8,128)S(1)} collective-permute-done((f32[3,16,128]{2,1,0:T(8,128)S(1)}, f32[3,16,128]{2,1,0:T(8,128)S(1)}, u32[]{:S(2)}, u32[]{:S(2)}) %collective-permute-start.3) | collective-permute-done | bytes 24608 | tf_op jit(solution)/shard_map/ppermute | solution.py:111
  57.3 3.5 %collective-permute-done.2.dip_ref = f32[3,24,128]{2,1,0:T(8,128)S(1)} collective-permute-done((f32[3,24,128]{2,1,0:T(8,128)S(1)}, f32[3,24,128]{2,1,0:T(8,128)S(1)}, u32[]{:S(2)}, u32[]{:S(2)}) %collective-permute-start.2) | collective-permute-done | bytes 36896 | tf_op jit(solution)/shard_map/ppermute | solution.py:113
  60.9 0.0 collective-permute-done.4.corner_ref
  60.9 0.0 copy-done.3
  60.9 0.8 %update.1 = (f32[3,8,16,128]{3,2,1,0:T(8,128)}, f32[3,8,16,128]{3,2,1,0:T(8,128)}) custom-call(f32[3,8,16,128]{3,2,1,0:T(8,128)S(1)} %copy-done.1, f32[3,8,16,128]{3,2,1,0:T(8,128)S(1)} %copy-done.2, f32[8,16,128]{2,1,0:T(8,128)S(1)} %copy-done.3, f32[3,8,16,128]{3,2,1,0:T(8,128)S(1)} %get-tuple-element.18.force_ref, ...), custom_call_target="tpu_custom_call" | custom-call | tf_op jit(solution)/shard_map/update/pallas_call | solution.py:600
  (8 shorter events, 0.0 us)
Async XLA Ops:
  1.4 21.7 %collective-permute-start = (f32[6,16,128]{2,1,0:T(8,128)S(1)}, f32[6,16,128]{2,1,0:T(8,128)S(1)}, u32[]{:S(2)}, u32[]{:S(2)}) collective-permute-start(f32[6,16,128]{2,1,0:T(8,128)S(1)} %pad_maximum_fusion), channel_id=1, source_target_pairs={{0,120},{8,0},{16,8},{24,16},{32,24},{40,32},{48,40},{56,48},{64,5... | collective-permute-start | bytes 147464 | tf_op jit(solution)/shard_map/ppermute | solution.py:111
  2.9 29.9 %copy-start.1 = (f32[3,8,16,128]{3,2,1,0:T(8,128)S(1)}, f32[3,8,16,128]{3,2,1,0:T(8,128)}, u32[]{:S(2)}) copy-start(f32[3,8,16,128]{3,2,1,0:T(8,128)} %disp_ref.1) | copy-start | bytes 589828
  2.9 29.9 %copy-start.4 = (f32[3,8,16,128]{3,2,1,0:T(8,128)S(1)}, f32[3,8,16,128]{3,2,1,0:T(8,128)}, u32[]{:S(2)}) copy-start(f32[3,8,16,128]{3,2,1,0:T(8,128)} %fwd_ref.1) | copy-start | bytes 589828
  2.9 29.9 %copy-start.5 = (f32[125,256]{1,0:T(8,128)S(1)}, f32[125,256]{1,0:T(8,128)}, u32[]{:S(2)}) copy-start(f32[125,256]{1,0:T(8,128)} %mu_ref.1) | copy-start | bytes 384004
  2.9 29.9 %copy-start.6 = (f32[125,256]{1,0:T(8,128)S(1)}, f32[125,256]{1,0:T(8,128)}, u32[]{:S(2)}) copy-start(f32[125,256]{1,0:T(8,128)} %kappa_ref.1) | copy-start | bytes 384004
  2.9 29.9 %copy-start.7 = (f32[2,4,32]{2,1,0:T(4,128)S(1)}, f32[2,4,32]{2,1,0:T(4,128)}, u32[]{:S(2)}) copy-start(f32[2,4,32]{2,1,0:T(4,128)} %shear_ref.1) | copy-start | bytes 3076
  2.9 29.9 %copy-start.8 = (f32[2,4,32]{2,1,0:T(4,128)S(1)}, f32[2,4,32]{2,1,0:T(4,128)}, u32[]{:S(2)}) copy-start(f32[2,4,32]{2,1,0:T(4,128)} %lame_ref.1) | copy-start | bytes 3076
  2.9 29.9 %copy-start.9 = (bf16[768,384]{1,0:T(8,128)(2,1)S(1)}, bf16[768,384]{1,0:T(8,128)(2,1)}, u32[]{:S(2)}) copy-start(bf16[768,384]{1,0:T(8,128)(2,1)} %constant.10.clone.table_ref) | copy-start | bytes 1769476
  12.4 25.1 %all-to-all-start = ((f32[128,8,128]{2,1,0:T(8,128)}), f32[128,8,128]{2,1,0:T(8,128)S(1)}, u32[]{:S(2)}, u32[]{:S(2)}) async-start(f32[128,8,128]{2,1,0:T(8,128)} %bitcast.13), calls=%async_computation | async-start | bytes 1048576 | tf_op jit(solution)/shard_map/all_to_all | solution.py:635
  23.9 13.6 %copy-start = (bf16[1248,512]{1,0:T(8,128)(2,1)S(1)}, bf16[1248,512]{1,0:T(8,128)(2,1)}, u32[]{:S(2)}) copy-start(bf16[1248,512]{1,0:T(8,128)(2,1)} %constant.11.clone.table_ref) | copy-start | bytes 3833860
  23.9 8.9 %collective-permute-start.1 = (f32[6,9,128]{2,1,0:T(8,128)S(1)}, f32[6,9,128]{2,1,0:T(8,128)S(1)}, u32[]{:S(2)}, u32[]{:S(2)}) collective-permute-start(f32[6,9,128]{2,1,0:T(8,128)S(1)} %pad_maximum_fusion.1), channel_id=1, source_target_pairs={{0,7},{1,0},{2,1},{3,2},{4,3},{5,4},{6,5},{7,6},{8,15},{9,8},{10,9... | collective-permute-start | bytes 82952 | tf_op jit(solution)/shard_map/ppermute | solution.py:113
  37.3 23.6 %copy-start.2 = (f32[3,8,16,128]{3,2,1,0:T(8,128)S(1)}, f32[3,8,16,128]{3,2,1,0:T(8,128)}, u32[]{:S(2)}) copy-start(f32[3,8,16,128]{3,2,1,0:T(8,128)} %veloc_ref.1) | copy-start | bytes 589828
  37.3 23.6 %copy-start.3 = (f32[8,16,128]{2,1,0:T(8,128)S(1)}, f32[8,16,128]{2,1,0:T(8,128)}, u32[]{:S(2)}) copy-start(f32[8,16,128]{2,1,0:T(8,128)} %mass_ref.1) | copy-start | bytes 196612
  51.7 9.2 %collective-permute-start.4 = (f32[3,32,128]{2,1,0:T(8,128)S(1)}, f32[3,32,128]{2,1,0:T(8,128)S(1)}, u32[]{:S(2)}, u32[]{:S(2)}) collective-permute-start(f32[3,32,128]{2,1,0:T(8,128)S(1)} %get-tuple-element.21), channel_id=1, source_target_pairs={{0,9},{1,10},{2,11},{3,12},{4,13},{5,14},{6,15},{7,8},{8,17},{9,18... | collective-permute-start | bytes 147464 | tf_op jit(solution)/shard_map/ppermute | solution.py:119
  54.1 6.7 %collective-permute-start.2 = (f32[3,24,128]{2,1,0:T(8,128)S(1)}, f32[3,24,128]{2,1,0:T(8,128)S(1)}, u32[]{:S(2)}, u32[]{:S(2)}) collective-permute-start(f32[3,24,128]{2,1,0:T(8,128)S(1)} %get-tuple-element.19), channel_id=1, source_target_pairs={{0,1},{1,2},{2,3},{3,4},{4,5},{5,6},{6,7},{7,0},{8,9},{9,10},{10,1... | collective-permute-start | bytes 110600 | tf_op jit(solution)/shard_map/ppermute | solution.py:113
  55.3 2.0 %collective-permute-start.3 = (f32[3,16,128]{2,1,0:T(8,128)S(1)}, f32[3,16,128]{2,1,0:T(8,128)S(1)}, u32[]{:S(2)}, u32[]{:S(2)}) collective-permute-start(f32[3,16,128]{2,1,0:T(8,128)S(1)} %get-tuple-element.20), channel_id=1, source_target_pairs={{0,8},{8,16},{16,24},{24,32},{32,40},{40,48},{48,56},{56,64},{64,7... | collective-permute-start | bytes 73736 | tf_op jit(solution)/shard_map/ppermute | solution.py:111
